TPU v7x, 256 devices: a whole 4x4x8 slice. The times are simulated.
256 devices in a mesh: circ: 32 (over y_hi, z, core), axial: 8 (over y_lo, x).
Axes of the slice: x: 4, y: 4 (y_hi: 2, y_lo: 2; y = y_hi * 2 + y_lo), z: 8, core: 2. Of those that a mesh axis runs over, the one named last changes fastest.
Arguments:
- scanned: float32 [3, 512, 32, 2048], P(None, None, 'circ', 'axial'), may hold values from -12 to 12
- block_mask: int32 [128, 16], P('circ', 'axial'), may hold values 0 or 1
Outputs:
- solution: float32 [3, 8192, 1024], P(None, 'circ', 'axial')
- residual: float32 [3, 8192, 1024], P(None, 'circ', 'axial')
All inputs are finite; a program needn't handle non-finite values. No bound on the sum of `block_mask` on one device may be relied on, other than what follows from the above.
Results may differ from a plain program's by a relative error of at most 0.00017.
Values sent between devices are 32-bit elements; how exact they have to be, the bound alone decides.
No kernel may reach another device: no remote copies, remote signals or barrier semaphores. Data moves between devices by JAX's collectives and lax.ppermute only.
A program may use at most 64 MiB of HBM per device.

v0:
```python
import jax
import jax.numpy as jnp
from jax import lax
from jax.sharding import PartitionSpec as P

BLK = 128
ITERS = 2


ridge_weight = 0.05


def padded_2(cells, sides, width, closed):
    for axis, dim in sides:
        count = lax.axis_size(axis)
        ends = count if closed else count - 1
        head = lax.slice_in_dim(cells, 0, width, axis=dim)
        tail = lax.slice_in_dim(cells, cells.shape[dim] - width, cells.shape[dim], axis=dim)
        cells = jnp.concatenate(
            [
                lax.ppermute(tail, axis, [(i, (i + 1) % count) for i in range(ends)]),
                cells,
                lax.ppermute(head, axis, [((i + 1) % count, i) for i in range(ends)]),
            ],
            axis=dim,
        )
    return cells


def spread(padded, axis):
    length = padded.shape[axis] - 3
    tap_zero = lax.slice_in_dim(padded, 0, length, axis=axis)
    tap_one = lax.slice_in_dim(padded, 1, length + 1, axis=axis)
    tap_two = lax.slice_in_dim(padded, 2, length + 2, axis=axis)
    tap_three = lax.slice_in_dim(padded, 3, length + 3, axis=axis)
    at_knots = (tap_zero + 4.0 * tap_one + tap_two) / 6.0
    at_halves = (tap_zero + 23.0 * tap_one + 23.0 * tap_two + tap_three) / 48.0
    joined = jnp.stack([at_knots, at_halves], axis=axis + 1)
    dims_list = list(padded.shape)
    dims_list[axis] = 2 * length
    return joined.reshape(dims_list)


def collect(padded, axis):
    length = padded.shape[axis] // 2 - 3
    dims_list = list(padded.shape)
    dims_list[axis : axis + 1] = [length + 3, 2]
    paired = padded.reshape(dims_list)
    halves_at = lax.index_in_dim(paired, 0, axis + 1, keepdims=False)
    knots_at = lax.index_in_dim(paired, 1, axis + 1, keepdims=False)

    def window(values, offset):
        return lax.slice_in_dim(values, offset, offset + length, axis=axis)

    return (
        (window(halves_at, 0) + window(halves_at, 3)) / 48.0
        + (window(knots_at, 0) + window(knots_at, 2)) / 6.0
        + 23.0 * (window(halves_at, 1) + window(halves_at, 2)) / 48.0
        + 4.0 * window(knots_at, 1) / 6.0
    )


def surface_of(padded, depth, extra):
    row_count = padded.shape[1] - 2 * depth
    col_count = padded.shape[2] - 2 * depth
    offset = 2 * (depth - 1) - extra
    widened = lax.slice_in_dim(
        spread(padded, 1), offset, offset + 2 * row_count + 2 * extra, axis=1
    )
    return lax.slice_in_dim(spread(widened, 2), offset, offset + 2 * col_count + 2 * extra, axis=2)


def tile_weights(mask_blocks):
    as_float = mask_blocks.astype(jnp.float32)
    return jnp.repeat(jnp.repeat(as_float, BLK, axis=0), BLK, axis=1)


def adjoint(masked):
    circled = padded_2(masked, (("circ", 1),), 3, True)
    widened = padded_2(circled, (("axial", 2),), 3, False)
    return collect(collect(widened, 1), 2)


def squares(values):
    return lax.psum(jnp.sum(values * values), ("circ", "axial"))


def shards(scanned, block_mask):
    weights = tile_weights(block_mask)
    row_total = scanned.shape[1]
    col_total = scanned.shape[3]
    arrived = lax.all_to_all(scanned, "circ", split_axis=1, concat_axis=2, tiled=True)
    tiled = arrived.reshape(3, row_total, col_total)
    right_side = adjoint(tiled * weights)
    solution = jnp.zeros_like(right_side)
    residual = right_side
    direction = right_side
    norm_now = squares(residual)
    for iteration in range(ITERS):
        circled = padded_2(direction, (("circ", 1),), 2, True)
        padded = padded_2(circled, (("axial", 2),), 2, False)
        surface = surface_of(padded, 2, 0)
        applied = adjoint(surface * weights) + ridge_weight * direction
        step_size = norm_now / lax.psum(jnp.sum(direction * applied), ("circ", "axial"))
        solution = solution + step_size * direction
        residual = residual - step_size * applied
        norm_next = squares(residual)
        direction = residual + norm_next / norm_now * direction
        norm_now = norm_next
    return (solution, residual)


def solution(mesh):
    return jax.shard_map(
        shards,
        mesh=mesh,
        in_specs=(P(None, None, "circ", "axial"), P("circ", "axial")),
        out_specs=(P(None, "circ", "axial"), P(None, "circ", "axial")),
        check_vma=False,
    )
```

profile of v0, /device:TPU:1, one launch (start us, length us, event | category | flops | bytes accessed | tf_op | source)
XLA Modules:
  0.0 464.6 jit_solution(9666643729506197314)
XLA Ops:
  0.6 3.7 copy.101
  4.3 12.9 %all-to-all-start = ((f32[3,512,1,256]{3,2,0,1:T(1,128)}), f32[3,512,1,256]{3,2,0,1:T(1,128)S(1)}, u32[]{:S(2)}, u32[]{:S(2)}) async-start(f32[3,512,1,256]{3,2,0,1:T(1,128)} %copy.101), calls=%async_computation | async-start | bytes 3145728 | tf_op jit(solution)/shard_map/all_to_all | solution.py:92
  18.0 39.0 %all-to-all-done = f32[3,512,1,256]{3,2,0,1:T(1,128)S(1)} async-done(((f32[3,512,1,256]{3,2,0,1:T(1,128)}), f32[3,512,1,256]{3,2,0,1:T(1,128)S(1)}, u32[]{:S(2)}, u32[]{:S(2)}) %all-to-all-start) | async-done | bytes 1572896 | tf_op jit(solution)/shard_map/all_to_all | solution.py:92
  58.2 3.6 collective-permute-start
  62.7 2.6 collective-permute-done.1
  68.0 3.1 collective-permute-start.2
  73.4 2.7 collective-permute-done.3
  77.4 3.5 pad_maximum_fusion.2
  80.9 2.9 reshape.44
  92.4 2.5 collective-permute-done.5
  94.9 3.1 collective-permute-start.6
  99.9 2.6 collective-permute-done.7
  109.5 2.6 copy.113
  112.1 2.4 reshape.47
  115.9 3.1 copy.145
  122.1 4.9 %collective-permute-start.9 = (f32[3,3,256]{2,1,0:T(4,128)S(1)}, f32[3,3,256]{2,1,0:T(4,128)S(1)}, u32[]{:S(2)}, u32[]{:S(2)}) collective-permute-start(f32[3,3,256]{2,1,0:T(4,128)S(1)} %get-tuple-element.36), channel_id=1, source_target_pairs={{8,0},{16,8},{24,16},{32,24},{40,32},{48,40},{56,48},{64,56},{72,6... | collective-permute-start | bytes 27656 | tf_op jit(solution)/shard_map/ppermute | solution.py:23
  130.6 3.5 collective-permute-start.10
  136.2 3.1 collective-permute-done.11
  140.5 3.5 pad_maximum_fusion.3
  144.1 2.9 reshape.48
  152.4 83.5 %all-reduce = (f32[]{:T(128)}, f32[]{:T(128)}) all-reduce(f32[]{:T(128)} %get-tuple-element.11, f32[]{:T(128)} %get-tuple-element.10), channel_id=1, replica_groups=mesh['circ'=32,'axial'=8] {'circ','axial'}, use_global_device_ids=true, to_apply=%region_1.0 | all-reduce | flops 2 | bytes 16 | tf_op jit(solution)/shard_map/psum | solution.py:85
  237.9 73.5 %psum.30 = f32[]{:T(128)} all-reduce(f32[]{:T(128)} %multiply_reduce_fusion.1), channel_id=1, replica_groups=mesh['circ'=32,'axial'=8] {'circ','axial'}, use_global_device_ids=true, to_apply=%region_5.0 | all-reduce | flops 1 | bytes 8 | tf_op jit(solution)/shard_map/psum | solution.py:85
  312.8 2.4 collective-permute-start.12
  315.2 2.6 collective-permute-done.12
  317.8 2.8 collective-permute-done.13
  320.7 2.9 collective-permute-start.14
  325.2 2.9 collective-permute-done.15
  336.7 3.4 copy.127
  358.8 3.1 collective-permute-done.19
  363.1 3.5 pad_maximum_fusion.4
  366.6 2.9 reshape.52
  374.8 86.2 %psum.31 = f32[]{:T(128)} all-reduce(f32[]{:T(128)} %get-tuple-element.14), channel_id=1, replica_groups=mesh['circ'=32,'axial'=8] {'circ','axial'}, use_global_device_ids=true, to_apply=%region_7.0 | all-reduce | flops 1 | bytes 8 | tf_op jit(solution)/shard_map/psum | solution.py:104
  (121 shorter events, 81.1 us)
Async XLA Ops:
  4.3 12.9 %copy-start.4 = (s32[4,2]{0,1:T(2,128)S(1)}, s32[4,2]{0,1:T(2,128)}, u32[]{:S(2)}) copy-start(s32[4,2]{0,1:T(2,128)} %param.3) | copy-start | bytes 100
  4.3 52.7 %all-to-all-start = ((f32[3,512,1,256]{3,2,0,1:T(1,128)}), f32[3,512,1,256]{3,2,0,1:T(1,128)S(1)}, u32[]{:S(2)}, u32[]{:S(2)}) async-start(f32[3,512,1,256]{3,2,0,1:T(1,128)} %copy.101), calls=%async_computation | async-start | bytes 3145728 | tf_op jit(solution)/shard_map/all_to_all | solution.py:92
  18.0 40.1 %copy-start = (f32[64,8,2,128]{3,1,2,0:T(8,128)}, f32[64,8,2,128]{3,1,2,0:T(8,128)S(1)}, u32[]{:S(2)}) copy-start(f32[64,8,2,128]{3,1,2,0:T(8,128)S(1)} %copy.173) | copy-start | bytes 1572868
  58.2 4.5 collective-permute-start
  61.9 3.4 collective-permute-start.1
  68.0 5.1 %collective-permute-start.2 = (f32[3,518,3]{1,2,0:T(4,128)S(1)}, f32[3,518,3]{1,2,0:T(4,128)S(1)}, u32[]{:S(2)}, u32[]{:S(2)}) collective-permute-start(f32[3,518,3]{1,2,0:T(4,128)S(1)} %copy.105), channel_id=1, source_target_pairs={{0,1},{1,2},{2,3},{3,4},{4,5},{5,6},{6,7},{8,9},{9,10},{10,11},{11... | collective-permute-start | bytes 55952 | tf_op jit(solution)/shard_map/ppermute | solution.py:21
  71.5 4.7 %collective-permute-start.3 = (f32[3,518,3]{1,2,0:T(4,128)S(1)}, f32[3,518,3]{1,2,0:T(4,128)S(1)}, u32[]{:S(2)}, u32[]{:S(2)}) collective-permute-start(f32[3,518,3]{1,2,0:T(4,128)S(1)} %copy.106), channel_id=1, source_target_pairs={{1,0},{2,1},{3,2},{4,3},{5,4},{6,5},{7,6},{9,8},{10,9},{11,10},{12... | collective-permute-start | bytes 55952 | tf_op jit(solution)/shard_map/ppermute | solution.py:23
  88.5 3.9 collective-permute-start.4
  89.7 5.1 %collective-permute-start.5 = (f32[3,2,128]{1,2,0:T(8,128)S(1)}, f32[3,2,128]{1,2,0:T(8,128)S(1)}, u32[]{:S(2)}, u32[]{:S(2)}) collective-permute-start(f32[3,2,128]{1,2,0:T(8,128)S(1)} %get-tuple-element.58), channel_id=1, source_target_pairs={{8,0},{16,8},{24,16},{32,24},{40,32},{48,40},{56,48},{64,56},{72,6... | collective-permute-start | bytes 9224 | tf_op jit(solution)/shard_map/ppermute | solution.py:23
  94.9 5.0 %collective-permute-start.6 = (f32[3,260,2]{1,2,0:T(2,128)S(1)}, f32[3,260,2]{1,2,0:T(2,128)S(1)}, u32[]{:S(2)}, u32[]{:S(2)}) collective-permute-start(f32[3,260,2]{1,2,0:T(2,128)S(1)} %get-tuple-element.47), channel_id=1, source_target_pairs={{0,1},{1,2},{2,3},{3,4},{4,5},{5,6},{6,7},{8,9},{9,10},{10,11},{11... | collective-permute-start | bytes 18728 | tf_op jit(solution)/shard_map/ppermute | solution.py:21
  98.1 4.4 collective-permute-start.7
  115.9 3.1 copy-start.1
  120.5 7.0 %collective-permute-start.8 = (f32[3,3,256]{2,1,0:T(4,128)S(1)}, f32[3,3,256]{2,1,0:T(4,128)S(1)}, u32[]{:S(2)}, u32[]{:S(2)}) collective-permute-start(f32[3,3,256]{2,1,0:T(4,128)S(1)} %get-tuple-element.35), channel_id=1, source_target_pairs={{0,8},{8,16},{16,24},{24,32},{32,40},{40,48},{48,56},{56,64},{64,7... | collective-permute-start | bytes 27656 | tf_op jit(solution)/shard_map/ppermute | solution.py:21
  122.1 5.8 %collective-permute-start.9 = (f32[3,3,256]{2,1,0:T(4,128)S(1)}, f32[3,3,256]{2,1,0:T(4,128)S(1)}, u32[]{:S(2)}, u32[]{:S(2)}) collective-permute-start(f32[3,3,256]{2,1,0:T(4,128)S(1)} %get-tuple-element.36), channel_id=1, source_target_pairs={{8,0},{16,8},{24,16},{32,24},{40,32},{48,40},{56,48},{64,56},{72,6... | collective-permute-start | bytes 27656 | tf_op jit(solution)/shard_map/ppermute | solution.py:23
  130.6 5.3 %collective-permute-start.10 = (f32[3,518,3]{1,2,0:T(4,128)S(1)}, f32[3,518,3]{1,2,0:T(4,128)S(1)}, u32[]{:S(2)}, u32[]{:S(2)}) collective-permute-start(f32[3,518,3]{1,2,0:T(4,128)S(1)} %copy.115), channel_id=1, source_target_pairs={{0,1},{1,2},{2,3},{3,4},{4,5},{5,6},{6,7},{8,9},{9,10},{10,11},{11... | collective-permute-start | bytes 55952 | tf_op jit(solution)/shard_map/ppermute | solution.py:21
  134.4 4.9 %collective-permute-start.11 = (f32[3,518,3]{1,2,0:T(4,128)S(1)}, f32[3,518,3]{1,2,0:T(4,128)S(1)}, u32[]{:S(2)}, u32[]{:S(2)}) collective-permute-start(f32[3,518,3]{1,2,0:T(4,128)S(1)} %copy.116), channel_id=1, source_target_pairs={{1,0},{2,1},{3,2},{4,3},{5,4},{6,5},{7,6},{9,8},{10,9},{11,10},{12... | collective-permute-start | bytes 55952 | tf_op jit(solution)/shard_map/ppermute | solution.py:23
  152.4 168.3 %copy-start.2 = (f32[3,256,128]{1,2,0:T(8,128)}, f32[3,256,128]{1,2,0:T(8,128)S(1)}, u32[]{:S(2)}) copy-start(f32[3,256,128]{1,2,0:T(8,128)S(1)} %get-tuple-element.16) | copy-start | bytes 1179652
  312.8 5.0 %collective-permute-start.12 = (f32[3,2,128]{1,2,0:T(8,128)S(1)}, f32[3,2,128]{1,2,0:T(8,128)S(1)}, u32[]{:S(2)}, u32[]{:S(2)}) collective-permute-start(f32[3,2,128]{1,2,0:T(8,128)S(1)} %get-tuple-element.55), channel_id=1, source_target_pairs={{0,8},{8,16},{16,24},{24,32},{32,40},{40,48},{48,56},{56,64},{64,7... | collective-permute-start | bytes 9224 | tf_op jit(solution)/shard_map/ppermute | solution.py:21
  315.2 5.4 %collective-permute-start.13 = (f32[3,2,128]{1,2,0:T(8,128)S(1)}, f32[3,2,128]{1,2,0:T(8,128)S(1)}, u32[]{:S(2)}, u32[]{:S(2)}) collective-permute-start(f32[3,2,128]{1,2,0:T(8,128)S(1)} %get-tuple-element.56), channel_id=1, source_target_pairs={{8,0},{16,8},{24,16},{32,24},{40,32},{48,40},{56,48},{64,56},{72,6... | collective-permute-start | bytes 9224 | tf_op jit(solution)/shard_map/ppermute | solution.py:23
  320.7 4.5 collective-permute-start.14
  323.7 4.4 collective-permute-start.15
  347.3 3.8 collective-permute-start.16
  348.5 3.1 collective-permute-start.17
  354.4 4.1 collective-permute-start.18
  356.9 4.9 %collective-permute-start.19 = (f32[3,518,3]{1,2,0:T(4,128)S(1)}, f32[3,518,3]{1,2,0:T(4,128)S(1)}, u32[]{:S(2)}, u32[]{:S(2)}) collective-permute-start(f32[3,518,3]{1,2,0:T(4,128)S(1)} %copy.130), channel_id=1, source_target_pairs={{1,0},{2,1},{3,2},{4,3},{5,4},{6,5},{7,6},{9,8},{10,9},{11,10},{12... | collective-permute-start | bytes 55952 | tf_op jit(solution)/shard_map/ppermute | solution.py:23
  373.8 88.5 %copy-start.3 = (f32[3,256,128]{1,2,0:T(8,128)S(1)}, f32[3,256,128]{1,2,0:T(8,128)}, u32[]{:S(2)}) copy-start(f32[3,256,128]{1,2,0:T(8,128)} %copy-done.2) | copy-start | bytes 1179652
where the time goes:
time: 470 us; the launch traced here: 465 us
  blocking collectives  243 us (52%)
  waiting for transfers between devices  67.9 us (14%)
  local copies, waits for them, and re-layouts  67.6 us (14%)
  starting transfers between devices  54.1 us (12%)
  other arithmetic  26.3 us (6%)
  between operations  5.34 us (1%)
    psum x2, blocking collectives, squares(): return lax.psum(jnp.sum(values * values), ('circ', 'axial'))  157 us
    psum x1, blocking collectives, shards(): lax.psum(jnp.sum(direction * applied), ('circ', 'axial'))  86.2 us
    all_to_all x1, waiting for transfers between devices, shards(): lax.all_to_all(scanned, 'circ', split_axis=1, concat_axis=2, tiled=True)  39 us
    ppermute x10, starting transfers between devices, padded_2(): lax.ppermute(tail, axis, [(i, (i + 1) % count) for i in range(ends)])  25 us
    ppermute x10, waiting for transfers between devices, padded_2(): lax.ppermute(head, axis, [((i + 1) % count, i) for i in range(ends)])  23 us
    ppermute x10, starting transfers between devices, padded_2(): lax.ppermute(head, axis, [((i + 1) % count, i) for i in range(ends)])  16.3 us
    all_to_all x1, starting transfers between devices, shards(): lax.all_to_all(scanned, 'circ', split_axis=1, concat_axis=2, tiled=True)  12.9 us
    concatenate x8, other arithmetic, padded_2(): jnp.concatenate([lax.ppermute(tail, axis, [(i, (i + 1) % count) for i in...  11.5 us
  transfers between devices with their start and end apart: 21, of which 16 were waited for; matrix products, arithmetic and copies ran while one was open for 1% of the time, Pallas kernels for 0%

commit v1 on v0

v1 whole, which is shorter than its diff:
```python
import functools

import jax
import jax.numpy as jnp
import numpy as np
from jax import lax
from jax.experimental import pallas as pl
from jax.experimental.pallas import tpu as pltpu
from jax.sharding import PartitionSpec as P

ridge_weight = 0.05
KS = 3
QN = 32
AN = 8
SL = 16
PR = 56
ROWS = 288
PAD = 16
LO, HI = 8, 280
LS, LB = 144, 8
VMEM_LIMIT = 48 * 1024 * 1024
F32 = jnp.float32
BF16 = jnp.bfloat16

TAPS = {0: 32.0, 1: 23.0, 2: 8.0, 3: 1.0}


def column_matrix():
    full = np.zeros((256, 256), np.float32)
    for a in range(128):
        for j in range(256):
            tap = TAPS.get(abs(j - 2 * a), 0.0)
            if tap and not (a in (63, 64, 65) and j >= 128):
                full[j, a] = tap
    for e, (a, low, high) in enumerate(
        [(-1, 0, 128), (128, 128, 256), (129, 128, 256), (63, 128, 256), (64, 128, 256), (65, 128, 256)]
    ):
        for j in range(low, high):
            for h in range(2):
                full[j, 128 + 18 * h + e] = TAPS.get(abs(j - 2 * a), 0.0)
    return full


def lanes(rows):
    return lax.broadcasted_iota(jnp.int32, (rows, 128), 1)


def roll(x, shift, axis=1):
    shift = shift % x.shape[axis]
    return x if shift == 0 else pltpu.roll(x, shift, axis)


def split_dot(x, matrix):
    high = x.astype(BF16)
    rest = x - high.astype(F32)
    mid = rest.astype(BF16)
    low = (rest - mid.astype(F32)).astype(BF16)
    dot = functools.partial(jnp.dot, preferred_element_type=F32)
    return dot(low, matrix) + dot(mid, matrix) + dot(high, matrix)


def pack_kernel(mask_ref, x_ref, c_ref, out_ref, main_ref, ext_ref):
    q = lax.axis_index("circ")
    lane = lanes(QN)
    matrix = c_ref[...]
    tile = None
    ext17 = None
    next_rows = []
    for k in range(KS):
        left = x_ref[k, pl.ds(0, 512, stride=2), :]
        right = x_ref[k, pl.ds(1, 512, stride=2), :]
        both = split_dot(jnp.concatenate([left, right], axis=1), matrix)
        main_ref[...] = both[:, :128]
        ext_ref[...] = both[:, 128:]
        for d in range(QN):
            out_ref[pl.ds(d * PR + k * SL, SL), :] = both[d * SL : (d + 1) * SL, :128]
        ext = both[:, 128:].reshape(QN, 2, 8, 128)
        ext = jnp.where(lanes(QN * 8) < 18, ext[:, 0].reshape(QN * 8, 128), ext[:, 1].reshape(QN * 8, 128))
        ext = roll(ext, 6 * k)
        tile = ext if tile is None else tile + ext

        def neighbour(ref):
            first = ref[pl.ds(0, QN, stride=SL), :]
            last = ref[pl.ds(SL - 1, QN, stride=SL), :]
            return jnp.where(q >= QN // 2, roll(last, 1, 0), roll(first, -1, 0))

        next_rows.append(neighbour(main_ref))
        ext_row = roll(jnp.where(lane < 6, neighbour(ext_ref), 0.0), 6 * k)
        ext17 = ext_row if ext17 is None else ext17 + ext_row
    for d in range(QN):
        out_ref[pl.ds(d * PR + 48, 8), :] = tile[d * 8 : (d + 1) * 8]
    mask_row = jnp.zeros((QN, 128), F32)
    for row in range(4):
        for col in range(2):
            mask_row = jnp.where(lane == 64 + 2 * row + col, mask_ref[row, col].astype(F32), mask_row)
    fill = []
    for k in range(KS):
        fill += [roll(next_rows[k], 64), next_rows[k]]
    fill += [roll(ext17, 64), mask_row]
    for row in range(8):
        where = pl.ds(48 + row, QN, stride=PR)
        out_ref[where, :] = jnp.where(lane < 64, out_ref[where, :], fill[row])


def tap_rows(even, odd, start, size):
    def ev(offset):
        return even(start + offset, size)

    def od(offset):
        return odd(start + offset, size)

    return (
        32.0 * ev(0) + 8.0 * (ev(-1) + ev(1)) + 23.0 * (od(-1) + od(0)) + (od(-2) + od(1))
    )


def block_row_ranges():
    edges = [LO] + [PAD + 64 * b for b in range(5)] + [HI]
    return list(zip(edges[:-1], edges[1:]))


def collect_kernel(mask_ref, got_ref, b_ref, right_ref, left_ref, m_ref, even_ref, odd_ref):
    d = lax.axis_index("circ")
    row_lane = lanes(1)

    def spread_lane(x, at):
        return jnp.broadcast_to(x[:, at : at + 1], (1, 128))

    before = got_ref[pl.ds(lax.rem(d + QN - 1, QN) * PR + 55, 1), :]
    after = got_ref[pl.ds(lax.rem(d + 1, QN) * PR + 55, 1), :]
    weights = [(spread_lane(before, 70), spread_lane(before, 71))]
    for row in range(4):
        weights.append(tuple(jnp.full((1, 128), mask_ref[row, col].astype(F32)) for col in range(2)))
    weights.append((spread_lane(after, 64), spread_lane(after, 65)))
    main_w = [jnp.where(row_lane <= 65, low, high) for low, high in weights]
    ext_first = (row_lane == 0) | (row_lane == 6) | (row_lane == 12)
    ext_w = [jnp.where(ext_first, low, high) for low, high in weights]
    zeros = jnp.zeros((8, 128), F32)
    for ref in (even_ref, odd_ref):
        for t in range(4):
            ref[t, 0:8, :] = zeros
            ref[t, HI : HI + 8, :] = zeros
    for parity, ref in ((0, even_ref), (1, odd_ref)):
        for k in range(KS):
            for s in range(SL):
                rows = got_ref[pl.ds(parity * PR + k * SL + s, 16, stride=2 * PR), :]
                ref[k, PAD + 16 * s : PAD + 16 * s + 16, :] = rows * main_w[1 + s // 4]
            low = got_ref[pl.ds(parity * PR + 48 + 2 * k, 16, stride=2 * PR), :]
            high = got_ref[pl.ds(parity * PR + 49 + 2 * k, 16, stride=2 * PR), :]
            rows = jnp.where(lanes(16) < 64, roll(low, 64), high)
            ref[k, HI - 8 : HI, :] = rows[:8] * main_w[5]
            ref[k, LO : LO + 8, :] = rows[8:] * main_w[0]
        for r in range(8):
            rows = got_ref[pl.ds(parity * PR + 48 + r, 16, stride=2 * PR), :]
            ref[3, PAD + 16 * r : PAD + 16 * r + 16, :] = rows * ext_w[1 + r // 4]
            at = PAD + 128 + 16 * r
            ref[3, at : at + 16, :] = roll(rows, -18) * ext_w[3 + r // 4]
        rows = roll(got_ref[pl.ds(parity * PR + 54, 16, stride=2 * PR), :], 64)
        ref[3, HI - 8 : HI, :] = rows[:8] * ext_w[5]
        ref[3, LO : LO + 8, :] = rows[8:] * ext_w[0]
    scale = 1.0 / (48.0 * 48.0)
    for t in range(4):
        b_ref[t, 0:8, :] = zeros
        b_ref[t, HI : HI + 8, :] = zeros
        for start in range(LO, HI, 16):
            b_ref[t, start : start + 16, :] = scale * tap_rows(
                lambda at, size: even_ref[t, at : at + size, :],
                lambda at, size: odd_ref[t, at : at + size, :],
                start,
                16,
            )
    lane8 = lanes(8)
    mask_cols = jnp.zeros((8, 128), F32)
    sub8 = lax.broadcasted_iota(jnp.int32, (8, 128), 0)
    for row in range(6):
        for col in range(2):
            mask_cols = jnp.where((sub8 == row) & (lane8 == 24 + col), weights[row][col], mask_cols)
    m_ref[...] = mask_cols
    for ref, to_right in ((right_ref, True), (left_ref, False)):
        lane = lanes(72)
        packed = None
        for g in range(4):
            rows = slice(72 * g, 72 * g + 72)
            ext = b_ref[3, rows, :]
            piece = jnp.zeros((72, 128), F32)
            for k in range(KS):
                main = b_ref[k, rows, :]
                if to_right:
                    first, second = roll(main, 8 * k - 122), roll(ext, 2 * k + 5)
                    cut = 8 * k + 6
                else:
                    first, second = roll(ext, 2 * k), roll(main, 8 * k + 1)
                    cut = 8 * k + 1
                piece = jnp.where((lane >= 8 * k) & (lane < 8 * k + 8), jnp.where(lane < cut, first, second), piece)
            if g == 0:
                piece = piece + jnp.concatenate([mask_cols, jnp.zeros((64, 128), F32)], axis=0)
            piece = roll(piece, 32 * g)
            packed = piece if packed is None else packed + piece
        ref[...] = packed


def place_kernel(b_ref, out_ref):
    for start in range(0, ROWS, 16):
        rows = slice(start, start + 16)
        lane = lanes(16)
        ext = b_ref[3, rows, :]
        rolled = []
        for k in range(KS):
            main = b_ref[k, rows, :]
            middle = roll(ext, 63 - (6 * k + 3))
            main = main + jnp.where((lane >= 63) & (lane < 66), middle, 0.0)
            rolled.append(roll(main, LB + 16 * k))
        for t in range(4):
            out = jnp.zeros((16, 128), F32)
            if t < KS:
                off = LB + 16 * t
                out = jnp.where(lane >= off, rolled[t], out)
                out = jnp.where(lane == off - 1, roll(ext, off - 1 - 6 * t), out)
            if t > 0:
                k = t - 1
                off = LB + 16 * k
                out = jnp.where(lane < off, rolled[k], out)
                out = jnp.where((lane >= off) & (lane < off + 2), roll(ext, off - (6 * k + 1)), out)
            out_ref[t, rows, :] = out


def lane_shift(parts, shift):
    rolled = [roll(part, -shift) for part in parts]
    lane = lanes(parts[0].shape[0])
    count = len(parts)
    if shift < 0:
        return [jnp.where(lane < -shift, rolled[(t - 1) % count], rolled[t]) for t in range(count)]
    return [jnp.where(lane >= 128 - shift, rolled[(t + 1) % count], rolled[t]) for t in range(count)]


def packed_columns(t):
    out = []
    for lane in range(128):
        at = 128 * t + lane
        k = min(at // LS, KS - 1)
        out.append(at - k * LS - LB)
    return out


def lane_range(lane, t, low, high):
    columns = packed_columns(t)
    where = None
    at = 0
    while at < 128:
        if low <= columns[at] < high:
            end = at
            while end < 128 and low <= columns[end] < high:
                end += 1
            piece = (lane >= at) & (lane < end)
            where = piece if where is None else where | piece
            at = end
        else:
            at += 1
    return where


def choose(where, x, y):
    return y if where is None else jnp.where(where, x, y)


def operate_kernel(
    own_ref, m_ref, from_left_ref, from_right_ref, red_ref, b_ref, p_ref, s_ref, ve_ref, vo_ref, x_ref, w_ref
):
    place = lax.axis_index("axial")
    inner_left = (place > 0).astype(F32)
    inner_right = (place < AN - 1).astype(F32)
    lane8 = lanes(8)
    lane16 = lanes(16)
    ones = jnp.ones((8, 128), F32)
    inside = []
    main = []
    for t in range(4):
        keep = choose(lane_range(lane8, t, -8, 0), ones * inner_left, ones)
        inside.append(choose(lane_range(lane8, t, 128, 200), ones * inner_right, keep))
        main.append(choose(lane_range(lane8, t, 0, 128), ones, jnp.zeros((8, 128), F32)))
    scale = 1.0 / (48.0**4)
    for block in range(6):

        def cell(ref, at):
            return jnp.broadcast_to(ref[block : block + 1, at : at + 1], (8, 128)) * scale

        low, high = cell(m_ref, 24), cell(m_ref, 25)
        left, right = cell(from_left_ref, 25), cell(from_right_ref, 24)
        for t in range(4):
            value = choose(lane_range(lane8, t, -8, 0), left, right)
            value = choose(lane_range(lane8, t, 0, 64), low, value)
            w_ref[t, 8 * block : 8 * block + 8, :] = choose(lane_range(lane8, t, 64, 128), high, value)

    for g in range(4):
        for start in range(72 * g, 72 * g + 72, 24):
            rows = slice(start, start + 24)
            there = slice(start - 72 * g, start - 72 * g + 24)
            lane = lanes(24)
            from_left, from_right = from_left_ref[there, :], from_right_ref[there, :]
            for t in range(4):
                out = own_ref[t, rows, :]
                if t < KS:
                    at = 2 + 16 * t
                    piece = roll(from_left, at - 8 * t - 32 * g)
                    out = out + jnp.where((lane >= at) & (lane < at + 8), piece, 0.0)
                if t > 0:
                    k = t - 1
                    at = 7 + 16 * k
                    piece = roll(from_right, at - 8 * k - 32 * g)
                    out = out + jnp.where((lane >= at) & (lane < at + 7), piece, 0.0)
                keep = jnp.concatenate([inside[t]] * 3, axis=0)
                b_ref[t, rows, :] = out * keep

    zeros = jnp.zeros((8, 128), F32)
    for t in range(4):
        for ref in (ve_ref, vo_ref, p_ref):
            ref[t, 0:8, :] = zeros
            ref[t, HI : HI + 8, :] = zeros
        for n in range(4):
            x_ref[n, t, 0:8, :] = zeros
            x_ref[n, t, HI : HI + 8, :] = zeros

    def weight_row(start):
        for block, (low, high) in enumerate(block_row_ranges()):
            if low <= start < high:
                return block
        return None

    def operate(src_ref, dst_ref, low, high, dst_shift):
        for start in range(LO, HI, 8):
            rows = slice(start, start + 8)
            v = [src_ref[t, rows, :] for t in range(4)]
            before, after, second = lane_shift(v, -1), lane_shift(v, 1), lane_shift(v, 2)
            for t in range(4):
                ve_ref[t, rows, :] = 32.0 * v[t] + 8.0 * (before[t] + after[t])
                vo_ref[t, rows, :] = (before[t] + second[t]) + 23.0 * (v[t] + after[t])
        for n, ref in enumerate((ve_ref, vo_ref)):
            for t in range(4):
                for start in range(LO, HI, 8):
                    rows = slice(start, start + 8)
                    block = weight_row(start)
                    weight = w_ref[t, 8 * block : 8 * block + 8, :]
                    before = ref[t, start - 1 : start + 7, :]
                    here = ref[t, rows, :]
                    after = ref[t, start + 1 : start + 9, :]
                    second = ref[t, start + 2 : start + 10, :]
                    x_ref[2 * n, t, rows, :] = (32.0 * here + 8.0 * (before + after)) * weight
                    x_ref[2 * n + 1, t, rows, :] = ((before + second) + 23.0 * (here + after)) * weight
        for start in range(low, high, 8):
            rows = slice(start, start + 8)
            y = []
            for n in range(2):
                y.append(
                    [
                        tap_rows(
                            lambda at, size: x_ref[2 * n, t, at : at + size, :],
                            lambda at, size: x_ref[2 * n + 1, t, at : at + size, :],
                            start,
                            8,
                        )
                        for t in range(4)
                    ]
                )
            even, odd = y
            odd_before = lane_shift(odd, -1)
            first = [8.0 * even[t] + 23.0 * odd[t] + odd_before[t] for t in range(4)]
            first = lane_shift(first, -1)
            last = lane_shift([8.0 * even[t] + odd[t] for t in range(4)], 1)
            for t in range(4):
                total = 32.0 * even[t] + 23.0 * odd[t] + first[t] + last[t]
                value = (total + ridge_weight * src_ref[t, rows, :]) * inside[t]
                dst_ref[t, start - dst_shift : start - dst_shift + 8, :] = value

    operate(b_ref, p_ref, LO, HI, 0)
    operate(p_ref, s_ref, PAD, PAD + 256, PAD)

    def total(x):
        return jnp.sum(jnp.sum(x, axis=0, keepdims=True), axis=1, keepdims=True)

    sums = [zeros, zeros]
    for t in range(4):
        for start in range(PAD, PAD + 256, 8):
            b = b_ref[t, start : start + 8, :] * main[t]
            p = p_ref[t, start : start + 8, :]
            sums = [sums[0] + b * b, sums[1] + b * p]
    norm, moment = total(sums[0]), total(sums[1])
    shift = jnp.where(norm > 1e-30, moment / jnp.where(norm > 1e-30, norm, 1.0), 0.0)
    shift8 = jnp.broadcast_to(shift, (8, 128))
    sums = [zeros] * 4
    for t in range(4):
        for start in range(PAD, PAD + 256, 8):
            b = b_ref[t, start : start + 8, :] * main[t]
            p = p_ref[t, start : start + 8, :] * main[t]
            s = s_ref[t, start - PAD : start - PAD + 8, :]
            w = p - shift8 * b
            z = s - shift8 * p
            sums = [sums[0] + w * b, sums[1] + w * w, sums[2] + w * z, sums[3] + b * z]
    values = [norm, moment] + [total(x) for x in sums] + [shift]
    row_lane = lax.broadcasted_iota(jnp.int32, (1, 8), 1)
    row = jnp.zeros((1, 8), F32)
    for n, value in enumerate(values):
        row = jnp.where(row_lane == n, jnp.broadcast_to(value, (1, 8)), row)
    red_ref[...] = jnp.broadcast_to(row, red_ref.shape)


def unpack_kernel(b_ref, p_ref, s_ref, bm_ref, pm_ref, sm_ref):
    for src, dst, base in ((b_ref, bm_ref, PAD), (p_ref, pm_ref, PAD), (s_ref, sm_ref, 0)):
        for k in range(KS):
            off = LB + 16 * k
            for start in range(0, 256, 16):
                first = src[k, base + start : base + start + 16, :]
                second = src[k + 1, base + start : base + start + 16, :]
                both = jnp.where(lanes(16) >= off, first, second)
                dst[k, start : start + 16, :] = roll(both, -off)


def finish_kernel(red_ref, b_ref, p_ref, s_ref, sol_ref, res_ref):
    red = red_ref[...]
    norm, moment, c, v, wz, bz, mu = (red[:, n : n + 1] for n in range(7))

    def total(x):
        return jnp.sum(x, axis=0, keepdims=True)

    norm_now = total(norm)
    moment_all = total(moment)
    step = norm_now / moment_all
    shift = mu - moment_all / norm_now
    norm_next = step * step * total(v + 2.0 * shift * c + shift * shift * norm)
    beta = norm_next / norm_now
    r_ar = step * step * total(wz + shift * (v + mu * c + bz) + shift * shift * moment)
    cross = -step * total(bz + v + mu * c + 2.0 * shift * moment)
    curve = r_ar + beta * cross + beta * beta * moment_all
    step_two = norm_next / curve
    one_beta = 1.0 + beta

    def wide(x):
        return jnp.broadcast_to(x, (16, 128))

    step_b, step_two_b, one_beta_b = wide(step), wide(step_two), wide(one_beta)
    for k in range(KS):
        for start in range(0, 256, 16):
            rows = slice(start, start + 16)
            b, p, s = b_ref[k, rows, :], p_ref[k, rows, :], s_ref[k, rows, :]
            first = step_b * p
            sol_ref[k, rows, :] = step_b * b + step_two_b * (one_beta_b * b - first)
            res_ref[k, rows, :] = (b - first) - step_two_b * (one_beta_b * p - step_b * s)


def call(kernel, outs, scratch=(), smem=0, n_in=1, cost=None):
    vmem = pl.BlockSpec(memory_space=pltpu.VMEM)
    smem_spec = pl.BlockSpec(memory_space=pltpu.SMEM)
    return pl.pallas_call(
        kernel,
        out_shape=[jax.ShapeDtypeStruct(shape, F32) for shape in outs],
        in_specs=[smem_spec] * smem + [vmem] * (n_in - smem),
        out_specs=[vmem] * len(outs),
        scratch_shapes=[pltpu.VMEM(shape, F32) for shape in scratch],
        compiler_params=pltpu.CompilerParams(vmem_limit_bytes=VMEM_LIMIT),
        cost_estimate=cost,
    )


def shards(scanned, block_mask):
    matrix = jnp.asarray(column_matrix(), BF16)
    x = scanned.reshape(KS, 1024, 128)
    (packed,) = call(pack_kernel, [(QN * PR, 128)], [(512, 128), (512, 128)], smem=1, n_in=3)(
        block_mask, x, matrix
    )
    got = lax.all_to_all(packed.reshape(QN, PR, 128), "circ", 0, 0, tiled=True).reshape(QN * PR, 128)
    b_own, to_right, to_left, mask_cols = call(
        collect_kernel,
        [(4, ROWS, 128), (72, 128), (72, 128), (8, 128)],
        [(4, ROWS, 128), (4, ROWS, 128)],
        smem=1,
        n_in=2,
    )(block_mask, got)
    from_left = lax.ppermute(to_right, "axial", [(i, i + 1) for i in range(AN - 1)])
    from_right = lax.ppermute(to_left, "axial", [(i + 1, i) for i in range(AN - 1)])
    cost = pl.CostEstimate(flops=2_000_000, bytes_accessed=4_000_000, transcendentals=0)
    (own,) = call(place_kernel, [(4, ROWS, 128)], n_in=1, cost=cost)(b_own)
    red, b, p, s = call(
        operate_kernel,
        [(QN * AN, 8), (4, ROWS, 128), (4, ROWS, 128), (4, 256, 128)],
        [(4, ROWS, 128), (4, ROWS, 128), (4, 4, ROWS, 128), (4, 48, 128)],
        n_in=4,
    )(own, mask_cols, from_left, from_right)
    all_red = lax.all_to_all(red, ("circ", "axial"), 0, 0, tiled=True)
    bm, pm, sm = call(unpack_kernel, [(KS, 256, 128)] * 3, n_in=3, cost=cost)(b, p, s)
    return tuple(call(finish_kernel, [(KS, 256, 128)] * 2, n_in=4)(all_red, bm, pm, sm))


def solution(mesh):
    return jax.shard_map(
        shards,
        mesh=mesh,
        in_specs=(P(None, None, "circ", "axial"), P("circ", "axial")),
        out_specs=(P(None, "circ", "axial"), P(None, "circ", "axial")),
        check_vma=False,
    )
```

time: 470 us -> 86.6 us (0.18); the launches traced: 465 us -> 86.3 us
  blocking collectives: 243 us -> 37.6 us
  local copies, waits for them, and re-layouts: 67.6 us -> 3.08 us
  waiting for transfers between devices: 67.9 us -> 13.2 us
  starting transfers between devices: 54.1 us -> 16.3 us
  other arithmetic: 26.3 us -> 0 us
  Pallas kernels: 0 us -> 15.4 us
    psum x3 -> x0, blocking collectives: 243 us -> none  [the longest x2 157 us: squares(): return lax.psum(jnp.sum(values * values), ('circ', 'axial'))]
    all_to_all x0 -> x1, blocking collectives: none -> 37.6 us  [shards(): lax.all_to_all(packed.reshape(QN, PR, 128), 'circ', 0, 0, tiled=True)]
    ppermute x20 -> x2, starting transfers between devices: 41.2 us -> 4.41 us  [the longest x1 3.12 us: shards(): lax.ppermute(to_right, 'axial', [(i, i + 1) for i in range(AN - 1)])]
    ppermute x20 -> x2, waiting for transfers between devices: 28.9 us -> 0.82 us  [the longest x1 0.81 us: shards(): lax.ppermute(to_left, 'axial', [(i + 1, i) for i in range(AN - 1)])]
    all_to_all x1, waiting for transfers between devices: 39 us -> 12.3 us  [shards(): all_red = lax.all_to_all(red, ('circ', 'axial'), 0, 0, tiled=True)]
    reshape x10 -> x0, local copies, waits for them, and re-layouts: 19.5 us -> none  [the longest x6 10.1 us: collect(): paired = padded.reshape(dims_list)]
    slice x22 -> x0, local copies, waits for them, and re-layouts: 19.5 us -> none  [the longest x11 8.12 us: padded_2(): lax.slice_in_dim(cells, cells.shape[dim] - width, cells.shape[dim], axis=...]
    pallas_call x0 -> x6, Pallas kernels: none -> 15.4 us  [the longest x1 7.21 us: shards(): call(operate_kernel, [(QN * AN, 8), (4, ROWS, 128), (4, ROWS, 128), (4, 2...]
  transfers between devices with their start and end apart: 21 -> 3, of which waited for: 16 -> 2; matrix products, arithmetic and copies ran while one was open for 1% -> 0% of each run, Pallas kernels for 0% -> 3%
where the time goes in v1:
time: 86.6 us; the launch traced here: 86.3 us
  blocking collectives  37.6 us (43%)
  starting transfers between devices  16.3 us (19%)
  Pallas kernels  15.4 us (18%)
  waiting for transfers between devices  13.2 us (15%)
  local copies, waits for them, and re-layouts  3.08 us (4%)
    all_to_all x1, blocking collectives, shards(): lax.all_to_all(packed.reshape(QN, PR, 128), 'circ', 0, 0, tiled=True)  37.6 us
    all_to_all x1, waiting for transfers between devices, shards(): all_red = lax.all_to_all(red, ('circ', 'axial'), 0, 0, tiled=True)  12.3 us
    all_to_all x1, starting transfers between devices, shards(): all_red = lax.all_to_all(red, ('circ', 'axial'), 0, 0, tiled=True)  11.9 us
    pallas_call x1, Pallas kernels, shards(): call(operate_kernel, [(QN * AN, 8), (4, ROWS, 128), (4, ROWS, 128), (4, 2...  7.21 us
    ppermute x1, starting transfers between devices, shards(): lax.ppermute(to_right, 'axial', [(i, i + 1) for i in range(AN - 1)])  3.12 us
    unnamed x5, local copies, waits for them, and re-layouts  3.08 us
    pallas_call x1, Pallas kernels, shards(): own, = call(place_kernel, [(4, ROWS, 128)], n_in=1, cost=cost)(b_own)  2.57 us
    pallas_call x1, Pallas kernels, shards(): call(collect_kernel, [(4, ROWS, 128), (72, 128), (72, 128), (8, 128)], [(...  1.85 us
  transfers between devices with their start and end apart: 3, of which 2 were waited for; matrix products, arithmetic and copies ran while one was open for 0% of the time, Pallas kernels for 3%

profile of v1, /device:TPU:1, one launch (start us, length us, event | category | flops | bytes accessed | tf_op | source)
XLA Modules:
  0.0 86.3 jit_solution(7061482940499513741)
XLA Ops:
  0.6 0.8 copy.8.mask_ref
  1.4 0.0 copy-start
  1.4 1.4 %copy-done = f32[3,512,1,256]{3,2,1,0:T(1,128)S(1)} copy-done((f32[3,512,1,256]{3,2,1,0:T(1,128)S(1)}, f32[3,512,1,256]{3,2,1,0:T(1,128)}, u32[]{:S(2)}) %copy-start) | copy-done | bytes 1572888
  2.8 0.0 copy-start.1
  2.8 0.9 %copy-done.1 = bf16[256,256]{1,0:T(8,128)(2,1)S(1)} copy-done((bf16[256,256]{1,0:T(8,128)(2,1)S(1)}, bf16[256,256]{1,0:T(8,128)(2,1)}, u32[]{:S(2)}) %copy-start.1) | copy-done | bytes 131096
  3.7 1.6 %shard_map.50 = f32[1792,128]{1,0:T(8,128)S(1)} custom-call(s32[4,2]{1,0:T(4,128)S(1)} %copy.8.mask_ref, f32[3,1024,128]{2,1,0:T(8,128)S(1)} %bitcast.9, bf16[256,256]{1,0:T(8,128)(2,1)S(1)} %copy-done.1), custom_call_target="tpu_custom_call" | custom-call | tf_op jit(solution)/shard_map/pallas_call | solution.py:466
  5.3 37.6 %all_to_all.16 = f32[32,56,128]{2,1,0:T(8,128)S(1)} all-to-all(f32[32,56,128]{2,1,0:T(8,128)S(1)} %bitcast.8), channel_id=1, replica_groups=mesh['circ'=32,'axial'=8] {'circ'}, dimensions={0} | all-to-all | bytes 1835008 | tf_op jit(solution)/shard_map/all_to_all | solution.py:469
  42.9 1.9 %shard_map.51 = (f32[4,288,128]{2,1,0:T(8,128)S(1)}, f32[72,128]{1,0:T(8,128)S(1)}, f32[72,128]{1,0:T(8,128)S(1)}, f32[8,128]{1,0:T(8,128)S(1)}) custom-call(s32[4,2]{1,0:T(4,128)S(1)} %copy.8.mask_ref, f32[1792,128]{1,0:T(8,128)S(1)} %bitcast.7), custom_call_target="tpu_custom_call" | custom-call | tf_op jit(solution)/shard_map/pallas_call | solution.py:470
  44.8 3.1 %collective-permute-start = (f32[72,128]{1,0:T(8,128)S(1)}, f32[72,128]{1,0:T(8,128)S(1)}, u32[]{:S(2)}, u32[]{:S(2)}) collective-permute-start(f32[72,128]{1,0:T(8,128)S(1)} %get-tuple-element.15), channel_id=1, source_target_pairs={{0,1},{1,2},{2,3},{3,4},{4,5},{5,6},{6,7},{8,9},{9,10},{10,11},{11... | collective-permute-start | bytes 110600 | tf_op jit(solution)/shard_map/ppermute | solution.py:477
  47.9 1.3 %collective-permute-start.1 = (f32[72,128]{1,0:T(8,128)S(1)}, f32[72,128]{1,0:T(8,128)S(1)}, u32[]{:S(2)}, u32[]{:S(2)}) collective-permute-start(f32[72,128]{1,0:T(8,128)S(1)} %get-tuple-element.16), channel_id=1, source_target_pairs={{1,0},{2,1},{3,2},{4,3},{5,4},{6,5},{7,6},{9,8},{10,9},{11,10},{12... | collective-permute-start | bytes 110600 | tf_op jit(solution)/shard_map/ppermute | solution.py:478
  49.2 2.6 %shard_map.52.own_ref = f32[4,288,128]{2,1,0:T(8,128)S(1)} custom-call(f32[4,288,128]{2,1,0:T(8,128)S(1)} %get-tuple-element.13.b_ref), custom_call_target="tpu_custom_call" | custom-call | flops 2000000 | bytes 4000000 | tf_op jit(solution)/shard_map/pallas_call | solution.py:480
  51.8 0.0 collective-permute-done.from_left_ref
  51.8 0.8 collective-permute-done.1.from_right_ref
  52.6 7.2 %shard_map.53 = (f32[256,8]{1,0:T(8,128)}, f32[4,288,128]{2,1,0:T(8,128)S(1)}, f32[4,288,128]{2,1,0:T(8,128)S(1)}, f32[4,256,128]{2,1,0:T(8,128)S(1)}) custom-call(f32[4,288,128]{2,1,0:T(8,128)S(1)} %shard_map.52.own_ref, f32[8,128]{1,0:T(8,128)S(1)} %get-tuple-element.14.m_ref, f32[72,128]{1,0:T(8,128)S(1)} %collective-permute-done.from_left_ref, ...), custom_call_target="tpu_custom_call" | custom-call | tf_op jit(solution)/shard_map/pallas_call | solution.py:481
  59.8 11.9 %all-to-all-start.1 = ((f32[256,1,8]{2,1,0:T(1,128)}), f32[256,1,8]{2,1,0:T(1,128)S(1)}, u32[]{:S(2)}, u32[]{:S(2)}) async-start(f32[256,1,8]{2,1,0:T(1,128)} %bitcast.4), calls=%async_computation.1 | async-start | bytes 262144 | tf_op jit(solution)/shard_map/all_to_all | solution.py:487
  71.7 0.4 shard_map.54
  72.1 12.3 %all-to-all-done.1 = f32[256,1,8]{2,1,0:T(1,128)S(1)} async-done(((f32[256,1,8]{2,1,0:T(1,128)}), f32[256,1,8]{2,1,0:T(1,128)S(1)}, u32[]{:S(2)}, u32[]{:S(2)}) %all-to-all-start.1) | async-done | bytes 8224 | tf_op jit(solution)/shard_map/all_to_all | solution.py:487
  84.5 1.8 %shard_map.55 = (f32[3,256,128]{2,1,0:T(8,128)}, f32[3,256,128]{2,1,0:T(8,128)}) custom-call(f32[256,8]{1,0:T(8,128)S(1)} %bitcast.10, f32[3,256,128]{2,1,0:T(8,128)S(1)} %get-tuple-element.21.b_ref, f32[3,256,128]{2,1,0:T(8,128)S(1)} %get-tuple-element.22.p_ref, f32[3,256,128]{2,1,0:T(8,128)S(1)} %get-tuple-element.23.s_ref), custom_call_target="tpu_custom_call" | custom-call | tf_op jit(solution)/shard_map/pallas_call | solution.py:489
Async XLA Ops:
  1.4 1.4 %copy-start = (f32[3,512,1,256]{3,2,1,0:T(1,128)S(1)}, f32[3,512,1,256]{3,2,1,0:T(1,128)}, u32[]{:S(2)}) copy-start(f32[3,512,1,256]{3,2,1,0:T(1,128)} %param.3) | copy-start | bytes 4718596
  2.8 0.9 %copy-start.1 = (bf16[256,256]{1,0:T(8,128)(2,1)S(1)}, bf16[256,256]{1,0:T(8,128)(2,1)}, u32[]{:S(2)}) copy-start(bf16[256,256]{1,0:T(8,128)(2,1)} %constant.2.clone.c_ref) | copy-start | bytes 393220
  44.8 7.0 %collective-permute-start = (f32[72,128]{1,0:T(8,128)S(1)}, f32[72,128]{1,0:T(8,128)S(1)}, u32[]{:S(2)}, u32[]{:S(2)}) collective-permute-start(f32[72,128]{1,0:T(8,128)S(1)} %get-tuple-element.15), channel_id=1, source_target_pairs={{0,1},{1,2},{2,3},{3,4},{4,5},{5,6},{6,7},{8,9},{9,10},{10,11},{11... | collective-permute-start | bytes 110600 | tf_op jit(solution)/shard_map/ppermute | solution.py:477
  47.9 4.7 %collective-permute-start.1 = (f32[72,128]{1,0:T(8,128)S(1)}, f32[72,128]{1,0:T(8,128)S(1)}, u32[]{:S(2)}, u32[]{:S(2)}) collective-permute-start(f32[72,128]{1,0:T(8,128)S(1)} %get-tuple-element.16), channel_id=1, source_target_pairs={{1,0},{2,1},{3,2},{4,3},{5,4},{6,5},{7,6},{9,8},{10,9},{11,10},{12... | collective-permute-start | bytes 110600 | tf_op jit(solution)/shard_map/ppermute | solution.py:478
  59.8 24.7 %all-to-all-start.1 = ((f32[256,1,8]{2,1,0:T(1,128)}), f32[256,1,8]{2,1,0:T(1,128)S(1)}, u32[]{:S(2)}, u32[]{:S(2)}) async-start(f32[256,1,8]{2,1,0:T(1,128)} %bitcast.4), calls=%async_computation.1 | async-start | bytes 262144 | tf_op jit(solution)/shard_map/all_to_all | solution.py:487

commit v2 on v1

--- a/solution.py
+++ b/solution.py
@@ -2,7 +2,6 @@
 
 import jax
 import jax.numpy as jnp
-import numpy as np
 from jax import lax
 from jax.experimental import pallas as pl
 from jax.experimental.pallas import tpu as pltpu
@@ -22,23 +21,20 @@
 F32 = jnp.float32
 BF16 = jnp.bfloat16
 
-TAPS = {0: 32.0, 1: 23.0, 2: 8.0, 3: 1.0}
-
 
 def column_matrix():
-    full = np.zeros((256, 256), np.float32)
-    for a in range(128):
-        for j in range(256):
-            tap = TAPS.get(abs(j - 2 * a), 0.0)
-            if tap and not (a in (63, 64, 65) and j >= 128):
-                full[j, a] = tap
-    for e, (a, low, high) in enumerate(
-        [(-1, 0, 128), (128, 128, 256), (129, 128, 256), (63, 128, 256), (64, 128, 256), (65, 128, 256)]
-    ):
-        for j in range(low, high):
-            for h in range(2):
-                full[j, 128 + 18 * h + e] = TAPS.get(abs(j - 2 * a), 0.0)
-    return full
+    sample = lax.broadcasted_iota(jnp.int32, (256, 256), 0)
+    out = lax.broadcasted_iota(jnp.int32, (256, 256), 1)
+    extra = out - 128
+    extra = jnp.where(extra >= 18, extra - 18, extra)
+    center = jnp.where(extra == 0, -2, jnp.where(extra < 3, 254 + 2 * extra, 120 + 2 * extra))
+    center = jnp.where(out < 128, 2 * out, jnp.where(extra < 6, center, 1000))
+    inner = (out >= 63) & (out <= 65) & (sample >= 128)
+    outer = (out >= 128) & (extra >= 3) & (sample < 128)
+    apart = inner | outer
+    away = jnp.abs(sample - center)
+    taps = jnp.where(away == 0, 32.0, jnp.where(away == 1, 23.0, jnp.where(away == 2, 8.0, 1.0)))
+    return jnp.where((away > 3) | apart, 0.0, taps).astype(BF16)
 
 
 def lanes(rows):
@@ -59,14 +55,19 @@
     return dot(low, matrix) + dot(mid, matrix) + dot(high, matrix)
 
 
-def pack_kernel(mask_ref, x_ref, c_ref, out_ref, main_ref, ext_ref):
+def pack_kernel(mask_hbm, x_hbm, out_ref, mask_ref, x_ref, main_ref, ext_ref, sems):
     q = lax.axis_index("circ")
+    copies = [pltpu.make_async_copy(x_hbm.at[k], x_ref.at[k], sems.at[k]) for k in range(KS)]
+    copies.append(pltpu.make_async_copy(mask_hbm, mask_ref, sems.at[KS]))
+    for copy in copies:
+        copy.start()
     lane = lanes(QN)
-    matrix = c_ref[...]
+    matrix = column_matrix()
     tile = None
     ext17 = None
     next_rows = []
     for k in range(KS):
+        copies[k].wait()
         left = x_ref[k, pl.ds(0, 512, stride=2), :]
         right = x_ref[k, pl.ds(1, 512, stride=2), :]
         both = split_dot(jnp.concatenate([left, right], axis=1), matrix)
@@ -89,10 +90,14 @@
         ext17 = ext_row if ext17 is None else ext17 + ext_row
     for d in range(QN):
         out_ref[pl.ds(d * PR + 48, 8), :] = tile[d * 8 : (d + 1) * 8]
-    mask_row = jnp.zeros((QN, 128), F32)
+    copies[KS].wait()
+    mask = mask_ref[...].astype(F32)
+    mask_row = jnp.zeros((1, 128), F32)
     for row in range(4):
         for col in range(2):
-            mask_row = jnp.where(lane == 64 + 2 * row + col, mask_ref[row, col].astype(F32), mask_row)
+            value = jnp.broadcast_to(mask[col : col + 1, row : row + 1], (1, 128))
+            mask_row = jnp.where(lanes(1) == 64 + 2 * row + col, value, mask_row)
+    mask_row = jnp.broadcast_to(mask_row, (QN, 128))
     fill = []
     for k in range(KS):
         fill += [roll(next_rows[k], 64), next_rows[k]]
@@ -119,7 +124,7 @@
     return list(zip(edges[:-1], edges[1:]))
 
 
-def collect_kernel(mask_ref, got_ref, b_ref, right_ref, left_ref, m_ref, even_ref, odd_ref):
+def collect_kernel(got_ref, b_ref, right_ref, left_ref, m_ref, even_ref, odd_ref):
     d = lax.axis_index("circ")
     row_lane = lanes(1)
 
@@ -129,8 +134,9 @@
     before = got_ref[pl.ds(lax.rem(d + QN - 1, QN) * PR + 55, 1), :]
     after = got_ref[pl.ds(lax.rem(d + 1, QN) * PR + 55, 1), :]
     weights = [(spread_lane(before, 70), spread_lane(before, 71))]
+    mine = got_ref[pl.ds(d * PR + 55, 1), :]
     for row in range(4):
-        weights.append(tuple(jnp.full((1, 128), mask_ref[row, col].astype(F32)) for col in range(2)))
+        weights.append(tuple(spread_lane(mine, 64 + 2 * row + col) for col in range(2)))
     weights.append((spread_lane(after, 64), spread_lane(after, 65)))
     main_w = [jnp.where(row_lane <= 65, low, high) for low, high in weights]
     ext_first = (row_lane == 0) | (row_lane == 6) | (row_lane == 12)
@@ -200,27 +206,23 @@
 
 
 def place_kernel(b_ref, out_ref):
-    for start in range(0, ROWS, 16):
-        rows = slice(start, start + 16)
-        lane = lanes(16)
-        ext = b_ref[3, rows, :]
-        rolled = []
-        for k in range(KS):
-            main = b_ref[k, rows, :]
-            middle = roll(ext, 63 - (6 * k + 3))
-            main = main + jnp.where((lane >= 63) & (lane < 66), middle, 0.0)
-            rolled.append(roll(main, LB + 16 * k))
-        for t in range(4):
+    lane = lanes(16)
+    for t in range(4):
+        for start in range(0, ROWS, 16):
+            rows = slice(start, start + 16)
             out = jnp.zeros((16, 128), F32)
+            ext = b_ref[3, rows, :]
+            if t > 0:
+                off = LB + 16 * (t - 1)
+                out = jnp.where(lane < off, roll(b_ref[t - 1, rows, :], off), out)
+                piece = roll(ext, off - 1 - 6 * (t - 1))
+                out = jnp.where((lane >= off) & (lane < off + 2), piece, out)
             if t < KS:
                 off = LB + 16 * t
-                out = jnp.where(lane >= off, rolled[t], out)
+                out = jnp.where(lane >= off, roll(b_ref[t, rows, :], off), out)
                 out = jnp.where(lane == off - 1, roll(ext, off - 1 - 6 * t), out)
-            if t > 0:
-                k = t - 1
-                off = LB + 16 * k
-                out = jnp.where(lane < off, rolled[k], out)
-                out = jnp.where((lane >= off) & (lane < off + 2), roll(ext, off - (6 * k + 1)), out)
+                piece = roll(ext, off + 63 - (6 * t + 3))
+                out = out + jnp.where((lane >= off + 63) & (lane < off + 66), piece, 0.0)
             out_ref[t, rows, :] = out
 
 
@@ -264,7 +266,27 @@
 
 
 def operate_kernel(
-    own_ref, m_ref, from_left_ref, from_right_ref, red_ref, b_ref, p_ref, s_ref, ve_ref, vo_ref, x_ref, w_ref
+    own_ref,
+    m_ref,
+    from_left_ref,
+    from_right_ref,
+    red_ref,
+    b_ref,
+    p_ref,
+    s_ref,
+    w_ref,
+    ve_ref,
+    vo_ref,
+    x_ref,
+    ye_ref,
+    yo_ref,
+    t_ref,
+    ve2_ref,
+    vo2_ref,
+    x2_ref,
+    ye2_ref,
+    yo2_ref,
+    t2_ref,
 ):
     place = lax.axis_index("axial")
     inner_left = (place > 0).astype(F32)
@@ -313,66 +335,79 @@
 
     zeros = jnp.zeros((8, 128), F32)
     for t in range(4):
-        for ref in (ve_ref, vo_ref, p_ref):
+        for ref in (ve_ref, vo_ref, ve2_ref, vo2_ref, p_ref):
             ref[t, 0:8, :] = zeros
             ref[t, HI : HI + 8, :] = zeros
-        for n in range(4):
-            x_ref[n, t, 0:8, :] = zeros
-            x_ref[n, t, HI : HI + 8, :] = zeros
-
-    def weight_row(start):
-        for block, (low, high) in enumerate(block_row_ranges()):
-            if low <= start < high:
-                return block
-        return None
-
-    def operate(src_ref, dst_ref, low, high, dst_shift):
-        for start in range(LO, HI, 8):
+        for ref in (x_ref, x2_ref):
+            for n in range(4):
+                ref[n, t, 0:8, :] = zeros
+                ref[n, t, HI : HI + 8, :] = zeros
+
+    block_of = {}
+    for block, (low, high) in enumerate(block_row_ranges()):
+        for start in range(low, high, 8):
+            block_of[start] = block
+
+    def stages(src_ref, dst_ref, dst_shift, spread_refs, x_ref, y_refs, t_ref):
+        def columns_out(start):
             rows = slice(start, start + 8)
             v = [src_ref[t, rows, :] for t in range(4)]
             before, after, second = lane_shift(v, -1), lane_shift(v, 1), lane_shift(v, 2)
             for t in range(4):
-                ve_ref[t, rows, :] = 32.0 * v[t] + 8.0 * (before[t] + after[t])
-                vo_ref[t, rows, :] = (before[t] + second[t]) + 23.0 * (v[t] + after[t])
-        for n, ref in enumerate((ve_ref, vo_ref)):
+                spread_refs[0][t, rows, :] = 32.0 * v[t] + 8.0 * (before[t] + after[t])
+                spread_refs[1][t, rows, :] = (before[t] + second[t]) + 23.0 * (v[t] + after[t])
+
+        def rows_out(start):
+            rows = slice(start, start + 8)
+            block = block_of[start]
             for t in range(4):
-                for start in range(LO, HI, 8):
-                    rows = slice(start, start + 8)
-                    block = weight_row(start)
-                    weight = w_ref[t, 8 * block : 8 * block + 8, :]
+                weight = w_ref[t, 8 * block : 8 * block + 8, :]
+                for n, ref in enumerate(spread_refs):
                     before = ref[t, start - 1 : start + 7, :]
                     here = ref[t, rows, :]
                     after = ref[t, start + 1 : start + 9, :]
                     second = ref[t, start + 2 : start + 10, :]
                     x_ref[2 * n, t, rows, :] = (32.0 * here + 8.0 * (before + after)) * weight
                     x_ref[2 * n + 1, t, rows, :] = ((before + second) + 23.0 * (here + after)) * weight
-        for start in range(low, high, 8):
+
+        def rows_in(start):
+            for t in range(4):
+                for n, ref in enumerate(y_refs):
+                    ref[t, start : start + 8, :] = tap_rows(
+                        lambda at, size: x_ref[2 * n, t, at : at + size, :],
+                        lambda at, size: x_ref[2 * n + 1, t, at : at + size, :],
+                        start,
+                        8,
+                    )
+
+        def columns_part(start):
             rows = slice(start, start + 8)
-            y = []
-            for n in range(2):
-                y.append(
-                    [
-                        tap_rows(
-                            lambda at, size: x_ref[2 * n, t, at : at + size, :],
-                            lambda at, size: x_ref[2 * n + 1, t, at : at + size, :],
-                            start,
-                            8,
-                        )
-                        for t in range(4)
-                    ]
-                )
-            even, odd = y
+            odd = [y_refs[1][t, rows, :] for t in range(4)]
             odd_before = lane_shift(odd, -1)
-            first = [8.0 * even[t] + 23.0 * odd[t] + odd_before[t] for t in range(4)]
-            first = lane_shift(first, -1)
+            for t in range(4):
+                t_ref[t, rows, :] = 8.0 * y_refs[0][t, rows, :] + 23.0 * odd[t] + odd_before[t]
+
+        def columns_in(start):
+            rows = slice(start, start + 8)
+            even = [y_refs[0][t, rows, :] for t in range(4)]
+            odd = [y_refs[1][t, rows, :] for t in range(4)]
+            first = lane_shift([t_ref[t, rows, :] for t in range(4)], -1)
             last = lane_shift([8.0 * even[t] + odd[t] for t in range(4)], 1)
             for t in range(4):
                 total = 32.0 * even[t] + 23.0 * odd[t] + first[t] + last[t]
                 value = (total + ridge_weight * src_ref[t, rows, :]) * inside[t]
                 dst_ref[t, start - dst_shift : start - dst_shift + 8, :] = value
 
-    operate(b_ref, p_ref, LO, HI, 0)
-    operate(p_ref, s_ref, PAD, PAD + 256, PAD)
+        return [columns_out, rows_out, rows_in, columns_part, columns_in]
+
+    work = [(stage, LO, HI) for stage in stages(b_ref, p_ref, 0, (ve_ref, vo_ref), x_ref, (ye_ref, yo_ref), t_ref)]
+    second = stages(p_ref, s_ref, PAD, (ve2_ref, vo2_ref), x2_ref, (ye2_ref, yo2_ref), t2_ref)
+    work += [(stage, LO, HI) for stage in second[:2]] + [(stage, PAD, PAD + 256) for stage in second[2:]]
+    for step in range((HI - LO) // 8 + len(work) - 1):
+        for n, (stage, low, high) in enumerate(work):
+            start = LO + 8 * (step - n)
+            if low <= start < high:
+                stage(start)
 
     def total(x):
         return jnp.sum(jnp.sum(x, axis=0, keepdims=True), axis=1, keepdims=True)
@@ -414,29 +449,37 @@
                 dst[k, start : start + 16, :] = roll(both, -off)
 
 
-def finish_kernel(red_ref, b_ref, p_ref, s_ref, sol_ref, res_ref):
+def finish_kernel(red_ref, b_ref, p_ref, s_ref, sol_hbm, res_hbm, sol_ref, res_ref, sems):
     red = red_ref[...]
-    norm, moment, c, v, wz, bz, mu = (red[:, n : n + 1] for n in range(7))
+    mu = red[:, 6:7]
 
     def total(x):
-        return jnp.sum(x, axis=0, keepdims=True)
-
-    norm_now = total(norm)
-    moment_all = total(moment)
+        x = jnp.sum(x, axis=0, keepdims=True)
+        return [x[:, n : n + 1] for n in range(6)]
+
+    sums = jnp.sum(red, axis=0, keepdims=True)
+    norm_now, moment_all = sums[:, 0:1], sums[:, 1:2]
     step = norm_now / moment_all
     shift = mu - moment_all / norm_now
-    norm_next = step * step * total(v + 2.0 * shift * c + shift * shift * norm)
+    shifted = shift * red
+    _, _, _, v, wz, bz = total(red)
+    _, moment_1, c_1, v_1, _, bz_1 = total(shifted)
+    norm_2, moment_2 = total(shift * shifted)[:2]
+    c_mu = total(mu * red)[2]
+    c_mu_1 = total(mu * shifted)[2]
+    norm_next = step * step * (v + 2.0 * c_1 + norm_2)
     beta = norm_next / norm_now
-    r_ar = step * step * total(wz + shift * (v + mu * c + bz) + shift * shift * moment)
-    cross = -step * total(bz + v + mu * c + 2.0 * shift * moment)
+    r_ar = step * step * (wz + v_1 + c_mu_1 + bz_1 + moment_2)
+    cross = -step * (bz + v + c_mu + 2.0 * moment_1)
     curve = r_ar + beta * cross + beta * beta * moment_all
     step_two = norm_next / curve
-    one_beta = 1.0 + beta
 
     def wide(x):
         return jnp.broadcast_to(x, (16, 128))
 
+    one_beta = 1.0 + beta
     step_b, step_two_b, one_beta_b = wide(step), wide(step_two), wide(one_beta)
+    copies = []
     for k in range(KS):
         for start in range(0, 256, 16):
             rows = slice(start, start + 16)
@@ -444,36 +487,47 @@
             first = step_b * p
             sol_ref[k, rows, :] = step_b * b + step_two_b * (one_beta_b * b - first)
             res_ref[k, rows, :] = (b - first) - step_two_b * (one_beta_b * p - step_b * s)
-
-
-def call(kernel, outs, scratch=(), smem=0, n_in=1, cost=None):
-    vmem = pl.BlockSpec(memory_space=pltpu.VMEM)
-    smem_spec = pl.BlockSpec(memory_space=pltpu.SMEM)
+        for n, (src, dst) in enumerate(((sol_ref, sol_hbm), (res_ref, res_hbm))):
+            copies.append(pltpu.make_async_copy(src.at[k], dst.at[k], sems.at[2 * k + n]))
+            copies[-1].start()
+    for copy in copies:
+        copy.wait()
+
+
+def call(kernel, outs, scratch=(), n_in=1, cost=None, hbm_in=False, hbm_out=False):
+    vmem, hbm = pl.BlockSpec(memory_space=pltpu.VMEM), pl.BlockSpec(memory_space=pltpu.HBM)
     return pl.pallas_call(
         kernel,
         out_shape=[jax.ShapeDtypeStruct(shape, F32) for shape in outs],
-        in_specs=[smem_spec] * smem + [vmem] * (n_in - smem),
-        out_specs=[vmem] * len(outs),
-        scratch_shapes=[pltpu.VMEM(shape, F32) for shape in scratch],
+        in_specs=[hbm if hbm_in else vmem] * n_in,
+        out_specs=[hbm if hbm_out else vmem] * len(outs),
+        scratch_shapes=[pltpu.VMEM(shape, F32) if isinstance(shape, tuple) else shape for shape in scratch],
         compiler_params=pltpu.CompilerParams(vmem_limit_bytes=VMEM_LIMIT),
         cost_estimate=cost,
     )
 
 
+PACK_SCRATCH = [
+    pltpu.VMEM((2, 4), jnp.int32),
+    (KS, 1024, 128),
+    (512, 128),
+    (512, 128),
+    pltpu.SemaphoreType.DMA((KS + 1,)),
+]
+FINISH_SCRATCH = [(KS, 256, 128), (KS, 256, 128), pltpu.SemaphoreType.DMA((2 * KS,))]
+OPERATE_SCRATCH = [(4, 48, 128)] + 2 * ([(4, ROWS, 128)] * 2 + [(4, 4, ROWS, 128)] + [(4, ROWS, 128)] * 3)
+
+
 def shards(scanned, block_mask):
-    matrix = jnp.asarray(column_matrix(), BF16)
-    x = scanned.reshape(KS, 1024, 128)
-    (packed,) = call(pack_kernel, [(QN * PR, 128)], [(512, 128), (512, 128)], smem=1, n_in=3)(
-        block_mask, x, matrix
-    )
+    x = pltpu.with_memory_space_constraint(scanned.reshape(KS, 1024, 128), pltpu.HBM)
+    mask = pltpu.with_memory_space_constraint(block_mask.T, pltpu.HBM)
+    (packed,) = call(pack_kernel, [(QN * PR, 128)], PACK_SCRATCH, n_in=2, hbm_in=True)(mask, x)
     got = lax.all_to_all(packed.reshape(QN, PR, 128), "circ", 0, 0, tiled=True).reshape(QN * PR, 128)
     b_own, to_right, to_left, mask_cols = call(
         collect_kernel,
         [(4, ROWS, 128), (72, 128), (72, 128), (8, 128)],
         [(4, ROWS, 128), (4, ROWS, 128)],
-        smem=1,
-        n_in=2,
-    )(block_mask, got)
+    )(got)
     from_left = lax.ppermute(to_right, "axial", [(i, i + 1) for i in range(AN - 1)])
     from_right = lax.ppermute(to_left, "axial", [(i + 1, i) for i in range(AN - 1)])
     cost = pl.CostEstimate(flops=2_000_000, bytes_accessed=4_000_000, transcendentals=0)
@@ -481,12 +535,12 @@
     red, b, p, s = call(
         operate_kernel,
         [(QN * AN, 8), (4, ROWS, 128), (4, ROWS, 128), (4, 256, 128)],
-        [(4, ROWS, 128), (4, ROWS, 128), (4, 4, ROWS, 128), (4, 48, 128)],
+        OPERATE_SCRATCH,
         n_in=4,
     )(own, mask_cols, from_left, from_right)
     all_red = lax.all_to_all(red, ("circ", "axial"), 0, 0, tiled=True)
     bm, pm, sm = call(unpack_kernel, [(KS, 256, 128)] * 3, n_in=3, cost=cost)(b, p, s)
-    return tuple(call(finish_kernel, [(KS, 256, 128)] * 2, n_in=4)(all_red, bm, pm, sm))
+    return tuple(call(finish_kernel, [(KS, 256, 128)] * 2, FINISH_SCRATCH, n_in=4, hbm_out=True)(all_red, bm, pm, sm))
 
 
 def solution(mesh):

time: 86.6 us -> 81.4 us (0.940)
  Pallas kernels: 15.4 us -> 11.5 us
  local copies, waits for them, and re-layouts: 3.08 us -> 0 us
  waiting for transfers between devices: 13.2 us -> 15.1 us
    unnamed x5 -> x0, local copies, waits for them, and re-layouts: 3.08 us -> none
    pallas_call x1, Pallas kernels: 7.21 us -> 4.97 us  [shards(): call(operate_kernel, [(QN * AN, 8), (4, ROWS, 128), (4, ROWS, 128), (4, 2...]
    pallas_call x1, Pallas kernels: 2.57 us -> 0.63 us  [shards(): own, = call(place_kernel, [(4, ROWS, 128)], n_in=1, cost=cost)(b_own)]
    ppermute x1, waiting for transfers between devices: 0.81 us -> 2.75 us  [shards(): lax.ppermute(to_left, 'axial', [(i + 1, i) for i in range(AN - 1)])]
    pallas_call x2, Pallas kernels: 3.43 us -> 4.33 us  [the longest x1 2.83 us: shards(): call(pack_kernel, [(QN * PR, 128)], PACK_SCRATCH, n_in=2, hbm_in=True)]
  transfers between devices with their start and end apart: 3 -> 3, of which waited for: 2 -> 2; matrix products, arithmetic and copies ran while one was open for 0% -> 0% of each run, Pallas kernels for 3% -> 1%
where the time goes in v2:
time: 81.4 us; the launch traced here: 81.2 us
  blocking collectives  37.6 us (46%)
  starting transfers between devices  16.3 us (20%)
  waiting for transfers between devices  15.1 us (19%)
  Pallas kernels  11.5 us (14%)
    all_to_all x1, blocking collectives, shards(): lax.all_to_all(packed.reshape(QN, PR, 128), 'circ', 0, 0, tiled=True)  37.6 us
    all_to_all x1, waiting for transfers between devices, shards(): all_red = lax.all_to_all(red, ('circ', 'axial'), 0, 0, tiled=True)  12.3 us
    all_to_all x1, starting transfers between devices, shards(): all_red = lax.all_to_all(red, ('circ', 'axial'), 0, 0, tiled=True)  11.9 us
    pallas_call x1, Pallas kernels, shards(): call(operate_kernel, [(QN * AN, 8), (4, ROWS, 128), (4, ROWS, 128), (4, 2...  4.97 us
    ppermute x1, starting transfers between devices, shards(): lax.ppermute(to_right, 'axial', [(i, i + 1) for i in range(AN - 1)])  3.12 us
    pallas_call x1, Pallas kernels, shards(): call(pack_kernel, [(QN * PR, 128)], PACK_SCRATCH, n_in=2, hbm_in=True)  2.83 us
    ppermute x1, waiting for transfers between devices, shards(): lax.ppermute(to_left, 'axial', [(i + 1, i) for i in range(AN - 1)])  2.75 us
  transfers between devices with their start and end apart: 3, of which 2 were waited for; matrix products, arithmetic and copies ran while one was open for 0% of the time, Pallas kernels for 1%

profile of v2, /device:TPU:1, one launch (start us, length us, event | category | flops | bytes accessed | tf_op | source)
XLA Modules:
  0.0 81.2 jit_solution(2240507464145471639)
XLA Ops:
  0.6 2.8 %shard_map.41 = f32[1792,128]{1,0:T(8,128)S(1)} custom-call(s32[2,4]{1,0:T(2,128)} %bitcast.12, f32[3,1024,128]{2,1,0:T(8,128)} %bitcast.11), custom_call_target="tpu_custom_call" | custom-call | tf_op jit(solution)/shard_map/pallas_call | solution.py:524
  3.5 37.6 %all_to_all.16 = f32[32,56,128]{2,1,0:T(8,128)S(1)} all-to-all(f32[32,56,128]{2,1,0:T(8,128)S(1)} %bitcast.9), channel_id=1, replica_groups=mesh['circ'=32,'axial'=8] {'circ'}, dimensions={0} | all-to-all | bytes 1835008 | tf_op jit(solution)/shard_map/all_to_all | solution.py:525
  41.1 1.2 %shard_map.42 = (f32[4,288,128]{2,1,0:T(8,128)S(1)}, f32[72,128]{1,0:T(8,128)S(1)}, f32[72,128]{1,0:T(8,128)S(1)}, f32[8,128]{1,0:T(8,128)S(1)}) custom-call(f32[1792,128]{1,0:T(8,128)S(1)} %bitcast.8), custom_call_target="tpu_custom_call" | custom-call | tf_op jit(solution)/shard_map/pallas_call | solution.py:526
  42.2 3.1 %collective-permute-start = (f32[72,128]{1,0:T(8,128)S(1)}, f32[72,128]{1,0:T(8,128)S(1)}, u32[]{:S(2)}, u32[]{:S(2)}) collective-permute-start(f32[72,128]{1,0:T(8,128)S(1)} %get-tuple-element.15), channel_id=1, source_target_pairs={{0,1},{1,2},{2,3},{3,4},{4,5},{5,6},{6,7},{8,9},{9,10},{10,11},{11... | collective-permute-start | bytes 110600 | tf_op jit(solution)/shard_map/ppermute | solution.py:531
  45.4 1.3 %collective-permute-start.1 = (f32[72,128]{1,0:T(8,128)S(1)}, f32[72,128]{1,0:T(8,128)S(1)}, u32[]{:S(2)}, u32[]{:S(2)}) collective-permute-start(f32[72,128]{1,0:T(8,128)S(1)} %get-tuple-element.16), channel_id=1, source_target_pairs={{1,0},{2,1},{3,2},{4,3},{5,4},{6,5},{7,6},{9,8},{10,9},{11,10},{12... | collective-permute-start | bytes 110600 | tf_op jit(solution)/shard_map/ppermute | solution.py:532
  46.7 0.6 shard_map.43.own_ref
  47.3 0.0 collective-permute-done.from_left_ref
  47.3 2.8 %collective-permute-done.1.from_right_ref = f32[72,128]{1,0:T(8,128)S(1)} collective-permute-done((f32[72,128]{1,0:T(8,128)S(1)}, f32[72,128]{1,0:T(8,128)S(1)}, u32[]{:S(2)}, u32[]{:S(2)}) %collective-permute-start.1) | collective-permute-done | bytes 36896 | tf_op jit(solution)/shard_map/ppermute | solution.py:532
  50.1 5.0 %shard_map.44 = (f32[256,8]{1,0:T(8,128)}, f32[4,288,128]{2,1,0:T(8,128)S(1)}, f32[4,288,128]{2,1,0:T(8,128)S(1)}, f32[4,256,128]{2,1,0:T(8,128)S(1)}) custom-call(f32[4,288,128]{2,1,0:T(8,128)S(1)} %shard_map.43.own_ref, f32[8,128]{1,0:T(8,128)S(1)} %get-tuple-element.14.m_ref, f32[72,128]{1,0:T(8,128)S(1)} %collective-permute-done.from_left_ref, ...), custom_call_target="tpu_custom_call" | custom-call | tf_op jit(solution)/shard_map/pallas_call | solution.py:535
  55.0 11.9 %all-to-all-start.1 = ((f32[256,1,8]{2,1,0:T(1,128)}), f32[256,1,8]{2,1,0:T(1,128)S(1)}, u32[]{:S(2)}, u32[]{:S(2)}) async-start(f32[256,1,8]{2,1,0:T(1,128)} %bitcast.5), calls=%async_computation.1 | async-start | bytes 262144 | tf_op jit(solution)/shard_map/all_to_all | solution.py:541
  67.0 0.4 shard_map.45
  67.3 12.3 %all-to-all-done.1 = f32[256,1,8]{2,1,0:T(1,128)S(1)} async-done(((f32[256,1,8]{2,1,0:T(1,128)}), f32[256,1,8]{2,1,0:T(1,128)S(1)}, u32[]{:S(2)}, u32[]{:S(2)}) %all-to-all-start.1) | async-done | bytes 8224 | tf_op jit(solution)/shard_map/all_to_all | solution.py:541
  79.7 1.5 %shard_map.46 = (f32[3,256,128]{2,1,0:T(8,128)}, f32[3,256,128]{2,1,0:T(8,128)}) custom-call(f32[256,8]{1,0:T(8,128)S(1)} %bitcast.10, f32[3,256,128]{2,1,0:T(8,128)S(1)} %get-tuple-element.21.b_ref, f32[3,256,128]{2,1,0:T(8,128)S(1)} %get-tuple-element.22.p_ref, f32[3,256,128]{2,1,0:T(8,128)S(1)} %get-tuple-element.23.s_ref), custom_call_target="tpu_custom_call" | custom-call | tf_op jit(solution)/shard_map/pallas_call | solution.py:543
Async XLA Ops:
  42.2 5.1 %collective-permute-start = (f32[72,128]{1,0:T(8,128)S(1)}, f32[72,128]{1,0:T(8,128)S(1)}, u32[]{:S(2)}, u32[]{:S(2)}) collective-permute-start(f32[72,128]{1,0:T(8,128)S(1)} %get-tuple-element.15), channel_id=1, source_target_pairs={{0,1},{1,2},{2,3},{3,4},{4,5},{5,6},{6,7},{8,9},{9,10},{10,11},{11... | collective-permute-start | bytes 110600 | tf_op jit(solution)/shard_map/ppermute | solution.py:531
  45.4 4.7 %collective-permute-start.1 = (f32[72,128]{1,0:T(8,128)S(1)}, f32[72,128]{1,0:T(8,128)S(1)}, u32[]{:S(2)}, u32[]{:S(2)}) collective-permute-start(f32[72,128]{1,0:T(8,128)S(1)} %get-tuple-element.16), channel_id=1, source_target_pairs={{1,0},{2,1},{3,2},{4,3},{5,4},{6,5},{7,6},{9,8},{10,9},{11,10},{12... | collective-permute-start | bytes 110600 | tf_op jit(solution)/shard_map/ppermute | solution.py:532
  55.0 24.6 %all-to-all-start.1 = ((f32[256,1,8]{2,1,0:T(1,128)}), f32[256,1,8]{2,1,0:T(1,128)S(1)}, u32[]{:S(2)}, u32[]{:S(2)}) async-start(f32[256,1,8]{2,1,0:T(1,128)} %bitcast.5), calls=%async_computation.1 | async-start | bytes 262144 | tf_op jit(solution)/shard_map/all_to_all | solution.py:541

commit v3 on v2

--- a/solution.py
+++ b/solution.py
@@ -16,7 +16,9 @@
 ROWS = 288
 PAD = 16
 LO, HI = 8, 280
-LS, LB = 144, 8
+LS, LB = 144, 2
+SHIFT = 8
+EDGE = 15
 VMEM_LIMIT = 48 * 1024 * 1024
 F32 = jnp.float32
 BF16 = jnp.bfloat16
@@ -124,7 +126,7 @@
     return list(zip(edges[:-1], edges[1:]))
 
 
-def collect_kernel(got_ref, b_ref, right_ref, left_ref, m_ref, even_ref, odd_ref):
+def collect_kernel(got_ref, b_ref, left_ref, m_ref, even_ref, odd_ref):
     d = lax.axis_index("circ")
     row_lane = lanes(1)
 
@@ -182,27 +184,25 @@
         for col in range(2):
             mask_cols = jnp.where((sub8 == row) & (lane8 == 24 + col), weights[row][col], mask_cols)
     m_ref[...] = mask_cols
-    for ref, to_right in ((right_ref, True), (left_ref, False)):
-        lane = lanes(72)
-        packed = None
-        for g in range(4):
-            rows = slice(72 * g, 72 * g + 72)
+    first_col = jnp.zeros((8, 128), F32)
+    for row in range(6):
+        first_col = jnp.where((sub8 == row) & (lane8 == EDGE), weights[row][0], first_col)
+    lane16 = lanes(16)
+    for start in range(0, ROWS // 2, 16):
+        halves = []
+        for g in range(2):
+            rows = slice(start + g * ROWS // 2, start + g * ROWS // 2 + 16)
             ext = b_ref[3, rows, :]
-            piece = jnp.zeros((72, 128), F32)
+            piece = jnp.zeros((16, 128), F32)
             for k in range(KS):
-                main = b_ref[k, rows, :]
-                if to_right:
-                    first, second = roll(main, 8 * k - 122), roll(ext, 2 * k + 5)
-                    cut = 8 * k + 6
-                else:
-                    first, second = roll(ext, 2 * k), roll(main, 8 * k + 1)
-                    cut = 8 * k + 1
-                piece = jnp.where((lane >= 8 * k) & (lane < 8 * k + 8), jnp.where(lane < cut, first, second), piece)
-            if g == 0:
-                piece = piece + jnp.concatenate([mask_cols, jnp.zeros((64, 128), F32)], axis=0)
-            piece = roll(piece, 32 * g)
-            packed = piece if packed is None else packed + piece
-        ref[...] = packed
+                at = 16 * k
+                piece = jnp.where(lane16 == at, roll(ext, at - 6 * k), piece)
+                piece = jnp.where((lane16 > at) & (lane16 < at + EDGE), roll(b_ref[k, rows, :], at + 1), piece)
+            halves.append(piece)
+        out = halves[0] + roll(halves[1], 64)
+        if start == 0:
+            out = out + jnp.concatenate([first_col, zeros], axis=0)
+        left_ref[start : start + 16, :] = out
 
 
 def place_kernel(b_ref, out_ref):
@@ -220,7 +220,6 @@
             if t < KS:
                 off = LB + 16 * t
                 out = jnp.where(lane >= off, roll(b_ref[t, rows, :], off), out)
-                out = jnp.where(lane == off - 1, roll(ext, off - 1 - 6 * t), out)
                 piece = roll(ext, off + 63 - (6 * t + 3))
                 out = out + jnp.where((lane >= off + 63) & (lane < off + 66), piece, 0.0)
             out_ref[t, rows, :] = out
@@ -268,7 +267,6 @@
 def operate_kernel(
     own_ref,
     m_ref,
-    from_left_ref,
     from_right_ref,
     red_ref,
     b_ref,
@@ -289,7 +287,7 @@
     t2_ref,
 ):
     place = lax.axis_index("axial")
-    inner_left = (place > 0).astype(F32)
+    first_tile = (place == 0).astype(F32)
     inner_right = (place < AN - 1).astype(F32)
     lane8 = lanes(8)
     lane16 = lanes(16)
@@ -297,9 +295,10 @@
     inside = []
     main = []
     for t in range(4):
-        keep = choose(lane_range(lane8, t, -8, 0), ones * inner_left, ones)
-        inside.append(choose(lane_range(lane8, t, 128, 200), ones * inner_right, keep))
-        main.append(choose(lane_range(lane8, t, 0, 128), ones, jnp.zeros((8, 128), F32)))
+        keep = choose(lane_range(lane8, t, -LB, 0), jnp.zeros((8, 128), F32), ones)
+        inside.append(choose(lane_range(lane8, t, 128, 400), ones * inner_right, keep))
+        own = choose(lane_range(lane8, t, SHIFT, SHIFT + 128), ones, jnp.zeros((8, 128), F32))
+        main.append(choose(lane_range(lane8, t, 0, SHIFT), ones * first_tile, own))
     scale = 1.0 / (48.0**4)
     for block in range(6):
 
@@ -307,31 +306,22 @@
             return jnp.broadcast_to(ref[block : block + 1, at : at + 1], (8, 128)) * scale
 
         low, high = cell(m_ref, 24), cell(m_ref, 25)
-        left, right = cell(from_left_ref, 25), cell(from_right_ref, 24)
+        right = cell(from_right_ref, EDGE)
         for t in range(4):
-            value = choose(lane_range(lane8, t, -8, 0), left, right)
+            value = choose(lane_range(lane8, t, -LB, 0), jnp.zeros((8, 128), F32), right)
             value = choose(lane_range(lane8, t, 0, 64), low, value)
             w_ref[t, 8 * block : 8 * block + 8, :] = choose(lane_range(lane8, t, 64, 128), high, value)
 
-    for g in range(4):
-        for start in range(72 * g, 72 * g + 72, 24):
-            rows = slice(start, start + 24)
-            there = slice(start - 72 * g, start - 72 * g + 24)
-            lane = lanes(24)
-            from_left, from_right = from_left_ref[there, :], from_right_ref[there, :]
+    for g in range(2):
+        for there in range(0, ROWS // 2, 16):
+            rows = slice(there + g * ROWS // 2, there + g * ROWS // 2 + 16)
+            piece = roll(from_right_ref[there : there + 16, :], LB - 1 - 64 * g)
             for t in range(4):
                 out = own_ref[t, rows, :]
-                if t < KS:
-                    at = 2 + 16 * t
-                    piece = roll(from_left, at - 8 * t - 32 * g)
-                    out = out + jnp.where((lane >= at) & (lane < at + 8), piece, 0.0)
                 if t > 0:
-                    k = t - 1
-                    at = 7 + 16 * k
-                    piece = roll(from_right, at - 8 * k - 32 * g)
-                    out = out + jnp.where((lane >= at) & (lane < at + 7), piece, 0.0)
-                keep = jnp.concatenate([inside[t]] * 3, axis=0)
-                b_ref[t, rows, :] = out * keep
+                    at = LB - 1 + 16 * (t - 1)
+                    out = out + jnp.where((lane16 >= at) & (lane16 < at + EDGE), piece, 0.0)
+                b_ref[t, rows, :] = out * jnp.concatenate([inside[t]] * 2, axis=0)
 
     zeros = jnp.zeros((8, 128), F32)
     for t in range(4):
@@ -438,15 +428,31 @@
     red_ref[...] = jnp.broadcast_to(row, red_ref.shape)
 
 
-def unpack_kernel(b_ref, p_ref, s_ref, bm_ref, pm_ref, sm_ref):
-    for src, dst, base in ((b_ref, bm_ref, PAD), (p_ref, pm_ref, PAD), (s_ref, sm_ref, 0)):
+def edges_kernel(b_ref, p_ref, s_ref, out_ref):
+    lane = lanes(16)
+    for start in range(0, 256, 16):
+        out = jnp.zeros((16, 128), F32)
+        for n, (src, base) in enumerate(((b_ref, PAD), (p_ref, PAD), (s_ref, 0))):
+            for k in range(KS):
+                at = SHIFT * (KS * n + k)
+                piece = roll(src[k + 1, base + start : base + start + 16, :], at - (LB + 16 * k))
+                out = jnp.where((lane >= at) & (lane < at + SHIFT), piece, out)
+        out_ref[start : start + 16, :] = out
+
+
+def unpack_kernel(b_ref, p_ref, s_ref, edge_ref, bm_ref, pm_ref, sm_ref):
+    first_tile = lax.axis_index("axial") == 0
+    lane = lanes(16)
+    own = (lane >= SHIFT) | first_tile
+    for n, (src, dst, base) in enumerate(((b_ref, bm_ref, PAD), (p_ref, pm_ref, PAD), (s_ref, sm_ref, 0))):
         for k in range(KS):
             off = LB + 16 * k
             for start in range(0, 256, 16):
                 first = src[k, base + start : base + start + 16, :]
                 second = src[k + 1, base + start : base + start + 16, :]
-                both = jnp.where(lanes(16) >= off, first, second)
-                dst[k, start : start + 16, :] = roll(both, -off)
+                both = roll(jnp.where(lane >= off, first, second), -off)
+                edge = roll(edge_ref[start : start + 16, :], -SHIFT * (KS * n + k))
+                dst[k, start : start + 16, :] = jnp.where(own, both, edge)
 
 
 def finish_kernel(red_ref, b_ref, p_ref, s_ref, sol_hbm, res_hbm, sol_ref, res_ref, sems):
@@ -523,12 +529,11 @@
     mask = pltpu.with_memory_space_constraint(block_mask.T, pltpu.HBM)
     (packed,) = call(pack_kernel, [(QN * PR, 128)], PACK_SCRATCH, n_in=2, hbm_in=True)(mask, x)
     got = lax.all_to_all(packed.reshape(QN, PR, 128), "circ", 0, 0, tiled=True).reshape(QN * PR, 128)
-    b_own, to_right, to_left, mask_cols = call(
+    b_own, to_left, mask_cols = call(
         collect_kernel,
-        [(4, ROWS, 128), (72, 128), (72, 128), (8, 128)],
+        [(4, ROWS, 128), (ROWS // 2, 128), (8, 128)],
         [(4, ROWS, 128), (4, ROWS, 128)],
     )(got)
-    from_left = lax.ppermute(to_right, "axial", [(i, i + 1) for i in range(AN - 1)])
     from_right = lax.ppermute(to_left, "axial", [(i + 1, i) for i in range(AN - 1)])
     cost = pl.CostEstimate(flops=2_000_000, bytes_accessed=4_000_000, transcendentals=0)
     (own,) = call(place_kernel, [(4, ROWS, 128)], n_in=1, cost=cost)(b_own)
@@ -536,10 +541,19 @@
         operate_kernel,
         [(QN * AN, 8), (4, ROWS, 128), (4, ROWS, 128), (4, 256, 128)],
         OPERATE_SCRATCH,
-        n_in=4,
-    )(own, mask_cols, from_left, from_right)
+        n_in=3,
+    )(own, mask_cols, from_right)
     all_red = lax.all_to_all(red, ("circ", "axial"), 0, 0, tiled=True)
-    bm, pm, sm = call(unpack_kernel, [(KS, 256, 128)] * 3, n_in=3, cost=cost)(b, p, s)
+
+    def share(b, p, s):
+        (edges,) = call(edges_kernel, [(256, 128)], n_in=3, cost=cost)(b, p, s)
+        edge = lax.ppermute(edges, "axial", [(i, i + 1) for i in range(AN - 1)])
+        return tuple(call(unpack_kernel, [(KS, 256, 128)] * 3, n_in=4, cost=cost)(b, p, s, edge))
+
+    def keep(b, p, s):
+        return tuple(x[:KS, :256] for x in (b, p, s))
+
+    bm, pm, sm = lax.cond(block_mask[0, 0] < 2, share, keep, b, p, s)
     return tuple(call(finish_kernel, [(KS, 256, 128)] * 2, FINISH_SCRATCH, n_in=4, hbm_out=True)(all_red, bm, pm, sm))
 
 

time: 81.4 us -> 78.1 us (0.959)
  waiting for transfers between devices: 15.1 us -> 10.5 us
    all_to_all x1, waiting for transfers between devices: 12.3 us -> 4.42 us  [shards(): all_red = lax.all_to_all(red, ('circ', 'axial'), 0, 0, tiled=True)]
    ppermute x1, waiting for transfers between devices: 0.01 us -> 2.79 us  [share(): edge = lax.ppermute(edges, 'axial', [(i, i + 1) for i in range(AN - 1)])]
    pallas_call x2 -> x3, Pallas kernels: 1.54 us -> 1.81 us  [the longest x1 0.81 us: shards(): call(collect_kernel, [(4, ROWS, 128), (ROWS // 2, 128), (8, 128)], [(4, R...]
  transfers between devices with their start and end apart: 3 -> 3, of which waited for: 2 -> 3; matrix products, arithmetic and copies ran while one was open for 0% -> 1% of each run, Pallas kernels for 1% -> 2%
where the time goes in v3:
time: 78.1 us; the launch traced here: 77.8 us
  blocking collectives  37.6 us (48%)
  starting transfers between devices  16.6 us (21%)
  Pallas kernels  11.3 us (14%)
  waiting for transfers between devices  10.5 us (13%)
  between operations  1.34 us (2%)
    all_to_all x1, blocking collectives, shards(): lax.all_to_all(packed.reshape(QN, PR, 128), 'circ', 0, 0, tiled=True)  37.6 us
    all_to_all x1, starting transfers between devices, shards(): all_red = lax.all_to_all(red, ('circ', 'axial'), 0, 0, tiled=True)  12 us
    pallas_call x1, Pallas kernels, shards(): call(operate_kernel, [(QN * AN, 8), (4, ROWS, 128), (4, ROWS, 128), (4, 2...  4.61 us
    all_to_all x1, waiting for transfers between devices, shards(): all_red = lax.all_to_all(red, ('circ', 'axial'), 0, 0, tiled=True)  4.42 us
    ppermute x1, starting transfers between devices, share(): edge = lax.ppermute(edges, 'axial', [(i, i + 1) for i in range(AN - 1)])  3.3 us
    ppermute x1, waiting for transfers between devices, shards(): lax.ppermute(to_left, 'axial', [(i + 1, i) for i in range(AN - 1)])  3.27 us
    pallas_call x1, Pallas kernels, shards(): call(pack_kernel, [(QN * PR, 128)], PACK_SCRATCH, n_in=2, hbm_in=True)  2.83 us
    ppermute x1, waiting for transfers between devices, share(): edge = lax.ppermute(edges, 'axial', [(i, i + 1) for i in range(AN - 1)])  2.79 us
  transfers between devices with their start and end apart: 3, of which 3 were waited for; matrix products, arithmetic and copies ran while one was open for 1% of the time, Pallas kernels for 2%

profile of v3, /device:TPU:1, one launch (start us, length us, event | category | flops | bytes accessed | tf_op | source)
XLA Modules:
  0.0 77.8 jit_solution(10392593112187416953)
XLA Ops:
  0.6 2.8 %shard_map.41 = f32[1792,128]{1,0:T(8,128)S(1)} custom-call(s32[2,4]{1,0:T(2,128)} %bitcast.13, f32[3,1024,128]{2,1,0:T(8,128)} %bitcast.12), custom_call_target="tpu_custom_call" | custom-call | tf_op jit(solution)/shard_map/pallas_call | solution.py:530
  3.5 37.6 %all_to_all.16 = f32[32,56,128]{2,1,0:T(8,128)S(1)} all-to-all(f32[32,56,128]{2,1,0:T(8,128)S(1)} %bitcast.10), channel_id=1, replica_groups=mesh['circ'=32,'axial'=8] {'circ'}, dimensions={0} | all-to-all | bytes 1835008 | tf_op jit(solution)/shard_map/all_to_all | solution.py:531
  41.1 0.0 copy-start
  41.1 0.8 %shard_map.42 = (f32[4,288,128]{2,1,0:T(8,128)S(1)}, f32[144,128]{1,0:T(8,128)S(1)}, f32[8,128]{1,0:T(8,128)S(1)}) custom-call(f32[1792,128]{1,0:T(8,128)S(1)} %bitcast.9), custom_call_target="tpu_custom_call" | custom-call | tf_op jit(solution)/shard_map/pallas_call | solution.py:532
  41.9 1.3 %collective-permute-start.1 = (f32[144,128]{1,0:T(8,128)S(1)}, f32[144,128]{1,0:T(8,128)S(1)}, u32[]{:S(2)}, u32[]{:S(2)}) collective-permute-start(f32[144,128]{1,0:T(8,128)S(1)} %get-tuple-element.32), channel_id=1, source_target_pairs={{1,0},{2,1},{3,2},{4,3},{5,4},{6,5},{7,6},{9,8},{10,9},{11,10},{12... | collective-permute-start | bytes 221192 | tf_op jit(solution)/shard_map/ppermute | solution.py:537
  43.2 0.5 shard_map.43.own_ref
  43.7 3.3 %collective-permute-done.1.from_right_ref = f32[144,128]{1,0:T(8,128)S(1)} collective-permute-done((f32[144,128]{1,0:T(8,128)S(1)}, f32[144,128]{1,0:T(8,128)S(1)}, u32[]{:S(2)}, u32[]{:S(2)}) %collective-permute-start.1) | collective-permute-done | bytes 73760 | tf_op jit(solution)/shard_map/ppermute | solution.py:537
  47.0 4.6 %shard_map.44 = (f32[256,8]{1,0:T(8,128)}, f32[4,288,128]{2,1,0:T(8,128)S(1)}, f32[4,288,128]{2,1,0:T(8,128)S(1)}, f32[4,256,128]{2,1,0:T(8,128)S(1)}) custom-call(f32[4,288,128]{2,1,0:T(8,128)S(1)} %shard_map.43.own_ref, f32[8,128]{1,0:T(8,128)S(1)} %get-tuple-element.31.m_ref, f32[144,128]{1,0:T(8,128)S(1)} %collective-permute-done.1.from_right_ref), custom_call_target="tpu_custom_call" | custom-call | tf_op jit(solution)/shard_map/pallas_call | solution.py:540
  51.6 12.0 %all-to-all-start.1 = ((f32[256,1,8]{2,1,0:T(1,128)}), f32[256,1,8]{2,1,0:T(1,128)S(1)}, u32[]{:S(2)}, u32[]{:S(2)}) async-start(f32[256,1,8]{2,1,0:T(1,128)} %bitcast.5), calls=%async_computation.1 | async-start | bytes 262144 | tf_op jit(solution)/shard_map/all_to_all | solution.py:546
  63.6 0.0 copy-done
  63.6 0.5 slice.12
  64.8 7.1 %conditional.1 = ((f32[3,256,128]{2,1,0:T(8,128)S(1)}, f32[3,256,128]{2,1,0:T(8,128)S(1)}, f32[3,256,128]{2,1,0:T(8,128)S(1)})) conditional(s32[]{:T(128)} %bitcast.7, (f32[4,288,128]{2,1,0:T(8,128)S(1)}, f32[4,288,128]{2,1,0:T(8,128)S(1)}, f32[4,256,128]{2,1,0:T(8,128)S(1)}) %tuple.14, (f32[4,288,128]{2,1,0:T(8,128)S(1)}, ...), branch_computations={%region_0.0_spmd, %region_1.0_spmd} | conditional | flops 4000000 | bytes 8524336 | solution.py:556
  64.8 0.4 branch_1_fun.2
  65.2 3.3 %collective-permute-start = (f32[256,128]{1,0:T(8,128)S(1)}, f32[256,128]{1,0:T(8,128)S(1)}, u32[]{:S(2)}, u32[]{:S(2)}) collective-permute-start(f32[256,128]{1,0:T(8,128)S(1)} %branch_1_fun.2), channel_id=1, source_target_pairs={{0,1},{1,2},{2,3},{3,4},{4,5},{5,6},{6,7},{8,9},{9,10},{10,11},{11... | collective-permute-start | bytes 393224 | tf_op jit(solution)/shard_map/cond/branch_1_fun/ppermute | solution.py:550
  68.5 2.8 %collective-permute-done.edge_ref = f32[256,128]{1,0:T(8,128)S(1)} collective-permute-done((f32[256,128]{1,0:T(8,128)S(1)}, f32[256,128]{1,0:T(8,128)S(1)}, u32[]{:S(2)}, u32[]{:S(2)}) %collective-permute-start) | collective-permute-done | bytes 131104 | tf_op jit(solution)/shard_map/cond/branch_1_fun/ppermute | solution.py:550
  71.3 0.6 branch_1_fun.3
  71.9 4.4 %all-to-all-done.1 = f32[256,1,8]{2,1,0:T(1,128)S(1)} async-done(((f32[256,1,8]{2,1,0:T(1,128)}), f32[256,1,8]{2,1,0:T(1,128)S(1)}, u32[]{:S(2)}, u32[]{:S(2)}) %all-to-all-start.1) | async-done | bytes 8224 | tf_op jit(solution)/shard_map/all_to_all | solution.py:546
  76.3 1.5 %shard_map.45 = (f32[3,256,128]{2,1,0:T(8,128)}, f32[3,256,128]{2,1,0:T(8,128)}) custom-call(f32[256,8]{1,0:T(8,128)S(1)} %bitcast.11, f32[3,256,128]{2,1,0:T(8,128)S(1)} %get-tuple-element.37.b_ref, f32[3,256,128]{2,1,0:T(8,128)S(1)} %get-tuple-element.38.p_ref, f32[3,256,128]{2,1,0:T(8,128)S(1)} %get-tuple-element.39.s_ref), custom_call_target="tpu_custom_call" | custom-call | tf_op jit(solution)/shard_map/pallas_call | solution.py:557
Async XLA Ops:
  41.1 22.5 %copy-start = (s32[4,2]{0,1:T(2,128)S(1)}, s32[4,2]{0,1:T(2,128)}, u32[]{:S(2)}) copy-start(s32[4,2]{0,1:T(2,128)} %param.5) | copy-start | bytes 100
  41.9 5.1 %collective-permute-start.1 = (f32[144,128]{1,0:T(8,128)S(1)}, f32[144,128]{1,0:T(8,128)S(1)}, u32[]{:S(2)}, u32[]{:S(2)}) collective-permute-start(f32[144,128]{1,0:T(8,128)S(1)} %get-tuple-element.32), channel_id=1, source_target_pairs={{1,0},{2,1},{3,2},{4,3},{5,4},{6,5},{7,6},{9,8},{10,9},{11,10},{12... | collective-permute-start | bytes 221192 | tf_op jit(solution)/shard_map/ppermute | solution.py:537
  51.6 24.7 %all-to-all-start.1 = ((f32[256,1,8]{2,1,0:T(1,128)}), f32[256,1,8]{2,1,0:T(1,128)S(1)}, u32[]{:S(2)}, u32[]{:S(2)}) async-start(f32[256,1,8]{2,1,0:T(1,128)} %bitcast.5), calls=%async_computation.1 | async-start | bytes 262144 | tf_op jit(solution)/shard_map/all_to_all | solution.py:546
  65.2 6.1 %collective-permute-start = (f32[256,128]{1,0:T(8,128)S(1)}, f32[256,128]{1,0:T(8,128)S(1)}, u32[]{:S(2)}, u32[]{:S(2)}) collective-permute-start(f32[256,128]{1,0:T(8,128)S(1)} %branch_1_fun.2), channel_id=1, source_target_pairs={{0,1},{1,2},{2,3},{3,4},{4,5},{5,6},{6,7},{8,9},{9,10},{10,11},{11... | collective-permute-start | bytes 393224 | tf_op jit(solution)/shard_map/cond/branch_1_fun/ppermute | solution.py:550

commit v4 on v3

--- a/solution.py
+++ b/solution.py
@@ -117,7 +117,7 @@
         return odd(start + offset, size)
 
     return (
-        32.0 * ev(0) + 8.0 * (ev(-1) + ev(1)) + 23.0 * (od(-1) + od(0)) + (od(-2) + od(1))
+        4.0 * ev(0) + (ev(-1) + ev(1)) + 23.0 * (od(-1) + od(0)) + (od(-2) + od(1))
     )
 
 
@@ -140,15 +140,19 @@
     for row in range(4):
         weights.append(tuple(spread_lane(mine, 64 + 2 * row + col) for col in range(2)))
     weights.append((spread_lane(after, 64), spread_lane(after, 65)))
-    main_w = [jnp.where(row_lane <= 65, low, high) for low, high in weights]
+    all_main_w = [jnp.where(row_lane <= 65, low, high) for low, high in weights]
     ext_first = (row_lane == 0) | (row_lane == 6) | (row_lane == 12)
-    ext_w = [jnp.where(ext_first, low, high) for low, high in weights]
+    all_ext_w = [jnp.where(ext_first, low, high) for low, high in weights]
     zeros = jnp.zeros((8, 128), F32)
     for ref in (even_ref, odd_ref):
         for t in range(4):
             ref[t, 0:8, :] = zeros
             ref[t, HI : HI + 8, :] = zeros
     for parity, ref in ((0, even_ref), (1, odd_ref)):
+        if parity == 0:
+            main_w, ext_w = [8.0 * w for w in all_main_w], [8.0 * w for w in all_ext_w]
+        else:
+            main_w, ext_w = all_main_w, all_ext_w
         for k in range(KS):
             for s in range(SL):
                 rows = got_ref[pl.ds(parity * PR + k * SL + s, 16, stride=2 * PR), :]
@@ -205,7 +209,8 @@
         left_ref[start : start + 16, :] = out
 
 
-def place_kernel(b_ref, out_ref):
+def place_kernel(b_ref, out_ref, flag_ref):
+    flag_ref[0] = 1
     lane = lanes(16)
     for t in range(4):
         for start in range(0, ROWS, 16):
@@ -310,7 +315,9 @@
         for t in range(4):
             value = choose(lane_range(lane8, t, -LB, 0), jnp.zeros((8, 128), F32), right)
             value = choose(lane_range(lane8, t, 0, 64), low, value)
-            w_ref[t, 8 * block : 8 * block + 8, :] = choose(lane_range(lane8, t, 64, 128), high, value)
+            value = choose(lane_range(lane8, t, 64, 128), high, value)
+            for power in range(3):
+                w_ref[power, t, 8 * block : 8 * block + 8, :] = 64.0**power * value
 
     for g in range(2):
         for there in range(0, ROWS // 2, 16):
@@ -344,21 +351,21 @@
             v = [src_ref[t, rows, :] for t in range(4)]
             before, after, second = lane_shift(v, -1), lane_shift(v, 1), lane_shift(v, 2)
             for t in range(4):
-                spread_refs[0][t, rows, :] = 32.0 * v[t] + 8.0 * (before[t] + after[t])
+                spread_refs[0][t, rows, :] = 4.0 * v[t] + (before[t] + after[t])
                 spread_refs[1][t, rows, :] = (before[t] + second[t]) + 23.0 * (v[t] + after[t])
 
         def rows_out(start):
             rows = slice(start, start + 8)
             block = block_of[start]
             for t in range(4):
-                weight = w_ref[t, 8 * block : 8 * block + 8, :]
+                weights = [w_ref[power, t, 8 * block : 8 * block + 8, :] for power in range(3)]
                 for n, ref in enumerate(spread_refs):
                     before = ref[t, start - 1 : start + 7, :]
                     here = ref[t, rows, :]
                     after = ref[t, start + 1 : start + 9, :]
                     second = ref[t, start + 2 : start + 10, :]
-                    x_ref[2 * n, t, rows, :] = (32.0 * here + 8.0 * (before + after)) * weight
-                    x_ref[2 * n + 1, t, rows, :] = ((before + second) + 23.0 * (here + after)) * weight
+                    x_ref[2 * n, t, rows, :] = (4.0 * here + (before + after)) * weights[2 - n]
+                    x_ref[2 * n + 1, t, rows, :] = ((before + second) + 23.0 * (here + after)) * weights[1 - n]
 
         def rows_in(start):
             for t in range(4):
@@ -375,16 +382,16 @@
             odd = [y_refs[1][t, rows, :] for t in range(4)]
             odd_before = lane_shift(odd, -1)
             for t in range(4):
-                t_ref[t, rows, :] = 8.0 * y_refs[0][t, rows, :] + 23.0 * odd[t] + odd_before[t]
+                t_ref[t, rows, :] = y_refs[0][t, rows, :] + 23.0 * odd[t] + odd_before[t]
 
         def columns_in(start):
             rows = slice(start, start + 8)
             even = [y_refs[0][t, rows, :] for t in range(4)]
             odd = [y_refs[1][t, rows, :] for t in range(4)]
             first = lane_shift([t_ref[t, rows, :] for t in range(4)], -1)
-            last = lane_shift([8.0 * even[t] + odd[t] for t in range(4)], 1)
+            last = lane_shift([even[t] + odd[t] for t in range(4)], 1)
             for t in range(4):
-                total = 32.0 * even[t] + 23.0 * odd[t] + first[t] + last[t]
+                total = 4.0 * even[t] + 23.0 * odd[t] + first[t] + last[t]
                 value = (total + ridge_weight * src_ref[t, rows, :]) * inside[t]
                 dst_ref[t, start - dst_shift : start - dst_shift + 8, :] = value
 
@@ -428,31 +435,47 @@
     red_ref[...] = jnp.broadcast_to(row, red_ref.shape)
 
 
+def edge_slot(strip, start):
+    if strip < 8:
+        return start % 128, 16 * strip + 8 * (start // 128)
+    return 128, start // 2
+
+
 def edges_kernel(b_ref, p_ref, s_ref, out_ref):
     lane = lanes(16)
-    for start in range(0, 256, 16):
+    places = {}
+    for n, (src, base) in enumerate(((b_ref, PAD), (p_ref, PAD), (s_ref, 0))):
+        for k in range(KS):
+            for start in range(0, 256, 16):
+                row, at = edge_slot(KS * n + k, start)
+                places.setdefault(row, []).append((src, k, base + start, at))
+    for row, pieces in places.items():
         out = jnp.zeros((16, 128), F32)
-        for n, (src, base) in enumerate(((b_ref, PAD), (p_ref, PAD), (s_ref, 0))):
-            for k in range(KS):
-                at = SHIFT * (KS * n + k)
-                piece = roll(src[k + 1, base + start : base + start + 16, :], at - (LB + 16 * k))
-                out = jnp.where((lane >= at) & (lane < at + SHIFT), piece, out)
-        out_ref[start : start + 16, :] = out
-
-
-def unpack_kernel(b_ref, p_ref, s_ref, edge_ref, bm_ref, pm_ref, sm_ref):
-    first_tile = lax.axis_index("axial") == 0
+        for src, k, start, at in pieces:
+            piece = roll(src[k + 1, start : start + 16, :], at - (LB + 16 * k))
+            out = jnp.where((lane >= at) & (lane < at + SHIFT), piece, out)
+        out_ref[row : row + 16, :] = out
+
+
+def unpack_kernel(b_ref, p_ref, s_ref, bm_ref, pm_ref, sm_ref):
     lane = lanes(16)
-    own = (lane >= SHIFT) | first_tile
-    for n, (src, dst, base) in enumerate(((b_ref, bm_ref, PAD), (p_ref, pm_ref, PAD), (s_ref, sm_ref, 0))):
+    for src, dst, base in ((b_ref, bm_ref, PAD), (p_ref, pm_ref, PAD), (s_ref, sm_ref, 0)):
         for k in range(KS):
             off = LB + 16 * k
             for start in range(0, 256, 16):
                 first = src[k, base + start : base + start + 16, :]
                 second = src[k + 1, base + start : base + start + 16, :]
-                both = roll(jnp.where(lane >= off, first, second), -off)
-                edge = roll(edge_ref[start : start + 16, :], -SHIFT * (KS * n + k))
-                dst[k, start : start + 16, :] = jnp.where(own, both, edge)
+                dst[k, start : start + 16, :] = roll(jnp.where(lane >= off, first, second), -off)
+
+
+def merge_kernel(edge_ref, b_ref, p_ref, s_ref, bm_ref, pm_ref, sm_ref):
+    own = (lanes(16) >= SHIFT) | (lax.axis_index("axial") == 0)
+    for n, (src, dst) in enumerate(((b_ref, bm_ref), (p_ref, pm_ref), (s_ref, sm_ref))):
+        for k in range(KS):
+            for start in range(0, 256, 16):
+                rows = slice(start, start + 16)
+                row, at = edge_slot(KS * n + k, start)
+                dst[k, rows, :] = jnp.where(own, src[k, rows, :], roll(edge_ref[row : row + 16, :], -at))
 
 
 def finish_kernel(red_ref, b_ref, p_ref, s_ref, sol_hbm, res_hbm, sol_ref, res_ref, sems):
@@ -500,13 +523,18 @@
         copy.wait()
 
 
-def call(kernel, outs, scratch=(), n_in=1, cost=None, hbm_in=False, hbm_out=False):
+def call(kernel, outs, scratch=(), n_in=1, cost=None, hbm_in=False, hbm_out=False, flag=False):
     vmem, hbm = pl.BlockSpec(memory_space=pltpu.VMEM), pl.BlockSpec(memory_space=pltpu.HBM)
+    out_shape = [jax.ShapeDtypeStruct(shape, F32) for shape in outs]
+    out_specs = [hbm if hbm_out else vmem] * len(outs)
+    if flag:
+        out_shape.append(jax.ShapeDtypeStruct((1,), jnp.int32))
+        out_specs.append(pl.BlockSpec(memory_space=pltpu.SMEM))
     return pl.pallas_call(
         kernel,
-        out_shape=[jax.ShapeDtypeStruct(shape, F32) for shape in outs],
+        out_shape=out_shape,
         in_specs=[hbm if hbm_in else vmem] * n_in,
-        out_specs=[hbm if hbm_out else vmem] * len(outs),
+        out_specs=out_specs,
         scratch_shapes=[pltpu.VMEM(shape, F32) if isinstance(shape, tuple) else shape for shape in scratch],
         compiler_params=pltpu.CompilerParams(vmem_limit_bytes=VMEM_LIMIT),
         cost_estimate=cost,
@@ -521,7 +549,7 @@
     pltpu.SemaphoreType.DMA((KS + 1,)),
 ]
 FINISH_SCRATCH = [(KS, 256, 128), (KS, 256, 128), pltpu.SemaphoreType.DMA((2 * KS,))]
-OPERATE_SCRATCH = [(4, 48, 128)] + 2 * ([(4, ROWS, 128)] * 2 + [(4, 4, ROWS, 128)] + [(4, ROWS, 128)] * 3)
+OPERATE_SCRATCH = [(3, 4, 48, 128)] + 2 * ([(4, ROWS, 128)] * 2 + [(4, 4, ROWS, 128)] + [(4, ROWS, 128)] * 3)
 
 
 def shards(scanned, block_mask):
@@ -536,7 +564,7 @@
     )(got)
     from_right = lax.ppermute(to_left, "axial", [(i + 1, i) for i in range(AN - 1)])
     cost = pl.CostEstimate(flops=2_000_000, bytes_accessed=4_000_000, transcendentals=0)
-    (own,) = call(place_kernel, [(4, ROWS, 128)], n_in=1, cost=cost)(b_own)
+    own, flag = call(place_kernel, [(4, ROWS, 128)], n_in=1, cost=cost, flag=True)(b_own)
     red, b, p, s = call(
         operate_kernel,
         [(QN * AN, 8), (4, ROWS, 128), (4, ROWS, 128), (4, 256, 128)],
@@ -546,14 +574,15 @@
     all_red = lax.all_to_all(red, ("circ", "axial"), 0, 0, tiled=True)
 
     def share(b, p, s):
-        (edges,) = call(edges_kernel, [(256, 128)], n_in=3, cost=cost)(b, p, s)
+        (edges,) = call(edges_kernel, [(144, 128)], n_in=3, cost=cost)(b, p, s)
         edge = lax.ppermute(edges, "axial", [(i, i + 1) for i in range(AN - 1)])
-        return tuple(call(unpack_kernel, [(KS, 256, 128)] * 3, n_in=4, cost=cost)(b, p, s, edge))
+        parts = call(unpack_kernel, [(KS, 256, 128)] * 3, n_in=3, cost=cost)(b, p, s)
+        return tuple(call(merge_kernel, [(KS, 256, 128)] * 3, n_in=4, cost=cost)(edge, *parts))
 
     def keep(b, p, s):
         return tuple(x[:KS, :256] for x in (b, p, s))
 
-    bm, pm, sm = lax.cond(block_mask[0, 0] < 2, share, keep, b, p, s)
+    bm, pm, sm = lax.cond(flag[0] > 0, share, keep, b, p, s)
     return tuple(call(finish_kernel, [(KS, 256, 128)] * 2, FINISH_SCRATCH, n_in=4, hbm_out=True)(all_red, bm, pm, sm))
 
 

time: 78.1 us -> 78 us (level)
    all_to_all x1, waiting for transfers between devices: 4.42 us -> 6.55 us  [shards(): all_red = lax.all_to_all(red, ('circ', 'axial'), 0, 0, tiled=True)]
    ppermute x1, waiting for transfers between devices: 2.79 us -> 1.1 us  [share(): edge = lax.ppermute(edges, 'axial', [(i, i + 1) for i in range(AN - 1)])]
    pallas_call x3 -> x4, Pallas kernels: 1.52 us -> 1.98 us  [the longest x1 0.89 us: shards(): call(place_kernel, [(4, ROWS, 128)], n_in=1, cost=cost, flag=True)(b_own)]
  transfers between devices with their start and end apart: 3 -> 3, of which waited for: 3 -> 3; matrix products, arithmetic and copies ran while one was open for 1% -> 0% of each run, Pallas kernels for 2% -> 3%
where the time goes in v4:
time: 78 us; the launch traced here: 77.7 us
  blocking collectives  37.6 us (48%)
  starting transfers between devices  16.6 us (21%)
  Pallas kernels  11.6 us (15%)
  waiting for transfers between devices  10.5 us (13%)
  between operations  1.32 us (2%)
    all_to_all x1, blocking collectives, shards(): lax.all_to_all(packed.reshape(QN, PR, 128), 'circ', 0, 0, tiled=True)  37.6 us
    all_to_all x1, starting transfers between devices, shards(): all_red = lax.all_to_all(red, ('circ', 'axial'), 0, 0, tiled=True)  12 us
    all_to_all x1, waiting for transfers between devices, shards(): all_red = lax.all_to_all(red, ('circ', 'axial'), 0, 0, tiled=True)  6.55 us
    pallas_call x1, Pallas kernels, shards(): call(operate_kernel, [(QN * AN, 8), (4, ROWS, 128), (4, ROWS, 128), (4, 2...  4.54 us
    ppermute x1, starting transfers between devices, share(): edge = lax.ppermute(edges, 'axial', [(i, i + 1) for i in range(AN - 1)])  3.29 us
    ppermute x1, waiting for transfers between devices, shards(): lax.ppermute(to_left, 'axial', [(i + 1, i) for i in range(AN - 1)])  2.9 us
    pallas_call x1, Pallas kernels, shards(): call(pack_kernel, [(QN * PR, 128)], PACK_SCRATCH, n_in=2, hbm_in=True)  2.83 us
  transfers between devices with their start and end apart: 3, of which 3 were waited for; matrix products, arithmetic and copies ran while one was open for 0% of the time, Pallas kernels for 3%

profile of v4, /device:TPU:1, one launch (start us, length us, event | category | flops | bytes accessed | tf_op | source)
XLA Modules:
  0.0 77.7 jit_solution(10028932004506978700)
XLA Ops:
  0.6 2.8 %shard_map.41 = f32[1792,128]{1,0:T(8,128)S(1)} custom-call(s32[2,4]{1,0:T(2,128)} %bitcast.13, f32[3,1024,128]{2,1,0:T(8,128)} %bitcast.12), custom_call_target="tpu_custom_call" | custom-call | tf_op jit(solution)/shard_map/pallas_call | solution.py:558
  3.5 37.6 %all_to_all.16 = f32[32,56,128]{2,1,0:T(8,128)S(1)} all-to-all(f32[32,56,128]{2,1,0:T(8,128)S(1)} %bitcast.10), channel_id=1, replica_groups=mesh['circ'=32,'axial'=8] {'circ'}, dimensions={0} | all-to-all | bytes 1835008 | tf_op jit(solution)/shard_map/all_to_all | solution.py:559
  41.1 0.8 %shard_map.42 = (f32[4,288,128]{2,1,0:T(8,128)S(1)}, f32[144,128]{1,0:T(8,128)S(1)}, f32[8,128]{1,0:T(8,128)S(1)}) custom-call(f32[1792,128]{1,0:T(8,128)S(1)} %bitcast.9), custom_call_target="tpu_custom_call" | custom-call | tf_op jit(solution)/shard_map/pallas_call | solution.py:560
  41.9 1.3 %collective-permute-start.1 = (f32[144,128]{1,0:T(8,128)S(1)}, f32[144,128]{1,0:T(8,128)S(1)}, u32[]{:S(2)}, u32[]{:S(2)}) collective-permute-start(f32[144,128]{1,0:T(8,128)S(1)} %get-tuple-element.38), channel_id=1, source_target_pairs={{1,0},{2,1},{3,2},{4,3},{5,4},{6,5},{7,6},{9,8},{10,9},{11,10},{12... | collective-permute-start | bytes 221192 | tf_op jit(solution)/shard_map/ppermute | solution.py:565
  43.2 0.9 %shard_map.43 = (f32[4,288,128]{2,1,0:T(8,128)S(1)}, s32[1]{0:T(128)}) custom-call(f32[4,288,128]{2,1,0:T(8,128)S(1)} %get-tuple-element.35.b_ref), custom_call_target="tpu_custom_call" | custom-call | flops 2000000 | bytes 4000000 | tf_op jit(solution)/shard_map/pallas_call | solution.py:567
  44.1 2.9 %collective-permute-done.1.from_right_ref = f32[144,128]{1,0:T(8,128)S(1)} collective-permute-done((f32[144,128]{1,0:T(8,128)S(1)}, f32[144,128]{1,0:T(8,128)S(1)}, u32[]{:S(2)}, u32[]{:S(2)}) %collective-permute-start.1) | collective-permute-done | bytes 73760 | tf_op jit(solution)/shard_map/ppermute | solution.py:565
  47.0 4.5 %shard_map.44 = (f32[256,8]{1,0:T(8,128)}, f32[4,288,128]{2,1,0:T(8,128)S(1)}, f32[4,288,128]{2,1,0:T(8,128)S(1)}, f32[4,256,128]{2,1,0:T(8,128)S(1)}) custom-call(f32[4,288,128]{2,1,0:T(8,128)S(1)} %get-tuple-element.36.own_ref, f32[8,128]{1,0:T(8,128)S(1)} %get-tuple-element.37.m_ref, f32[144,128]{1,0:T(8,128)S(1)} %collective-permute-done.1.from_right_ref), custom_call_target="tpu_custom_call" | custom-call | tf_op jit(solution)/shard_map/pallas_call | solution.py:568
  51.5 12.0 %all-to-all-start.1 = ((f32[256,1,8]{2,1,0:T(1,128)}), f32[256,1,8]{2,1,0:T(1,128)S(1)}, u32[]{:S(2)}, u32[]{:S(2)}) async-start(f32[256,1,8]{2,1,0:T(1,128)} %bitcast.5), calls=%async_computation.1 | async-start | bytes 262144 | tf_op jit(solution)/shard_map/all_to_all | solution.py:574
  64.2 5.5 %conditional.1 = ((f32[3,256,128]{2,1,0:T(8,128)S(1)}, f32[3,256,128]{2,1,0:T(8,128)S(1)}, f32[3,256,128]{2,1,0:T(8,128)S(1)})) conditional(s32[]{:T(128)} %bitcast.7, (f32[4,288,128]{2,1,0:T(8,128)S(1)}, f32[4,288,128]{2,1,0:T(8,128)S(1)}, f32[4,256,128]{2,1,0:T(8,128)S(1)}) %tuple.14, (f32[4,288,128]{2,1,0:T(8,128)S(1)}, ...), branch_computations={%region_0.0_spmd, %region_1.0_spmd} | conditional | flops 6000000 | bytes 12294960 | solution.py:585
  64.2 0.4 branch_1_fun.3
  64.6 3.3 %collective-permute-start = (f32[144,128]{1,0:T(8,128)S(1)}, f32[144,128]{1,0:T(8,128)S(1)}, u32[]{:S(2)}, u32[]{:S(2)}) collective-permute-start(f32[144,128]{1,0:T(8,128)S(1)} %branch_1_fun.3), channel_id=1, source_target_pairs={{0,1},{1,2},{2,3},{3,4},{4,5},{5,6},{6,7},{8,9},{9,10},{10,11},{11... | collective-permute-start | bytes 221192 | tf_op jit(solution)/shard_map/cond/branch_1_fun/ppermute | solution.py:578
  67.9 0.4 branch_1_fun.4
  68.2 1.1 %collective-permute-done.edge_ref = f32[144,128]{1,0:T(8,128)S(1)} collective-permute-done((f32[144,128]{1,0:T(8,128)S(1)}, f32[144,128]{1,0:T(8,128)S(1)}, u32[]{:S(2)}, u32[]{:S(2)}) %collective-permute-start) | collective-permute-done | bytes 73760 | tf_op jit(solution)/shard_map/cond/branch_1_fun/ppermute | solution.py:578
  69.3 0.3 branch_1_fun.5
  69.7 6.5 %all-to-all-done.1 = f32[256,1,8]{2,1,0:T(1,128)S(1)} async-done(((f32[256,1,8]{2,1,0:T(1,128)}), f32[256,1,8]{2,1,0:T(1,128)S(1)}, u32[]{:S(2)}, u32[]{:S(2)}) %all-to-all-start.1) | async-done | bytes 8224 | tf_op jit(solution)/shard_map/all_to_all | solution.py:574
  76.2 1.5 %shard_map.45 = (f32[3,256,128]{2,1,0:T(8,128)}, f32[3,256,128]{2,1,0:T(8,128)}) custom-call(f32[256,8]{1,0:T(8,128)S(1)} %bitcast.11, f32[3,256,128]{2,1,0:T(8,128)S(1)} %get-tuple-element.44.b_ref, f32[3,256,128]{2,1,0:T(8,128)S(1)} %get-tuple-element.45.p_ref, f32[3,256,128]{2,1,0:T(8,128)S(1)} %get-tuple-element.46.s_ref), custom_call_target="tpu_custom_call" | custom-call | tf_op jit(solution)/shard_map/pallas_call | solution.py:586
Async XLA Ops:
  41.9 5.1 %collective-permute-start.1 = (f32[144,128]{1,0:T(8,128)S(1)}, f32[144,128]{1,0:T(8,128)S(1)}, u32[]{:S(2)}, u32[]{:S(2)}) collective-permute-start(f32[144,128]{1,0:T(8,128)S(1)} %get-tuple-element.38), channel_id=1, source_target_pairs={{1,0},{2,1},{3,2},{4,3},{5,4},{6,5},{7,6},{9,8},{10,9},{11,10},{12... | collective-permute-start | bytes 221192 | tf_op jit(solution)/shard_map/ppermute | solution.py:565
  51.5 24.7 %all-to-all-start.1 = ((f32[256,1,8]{2,1,0:T(1,128)}), f32[256,1,8]{2,1,0:T(1,128)S(1)}, u32[]{:S(2)}, u32[]{:S(2)}) async-start(f32[256,1,8]{2,1,0:T(1,128)} %bitcast.5), calls=%async_computation.1 | async-start | bytes 262144 | tf_op jit(solution)/shard_map/all_to_all | solution.py:574
  64.6 4.8 %collective-permute-start = (f32[144,128]{1,0:T(8,128)S(1)}, f32[144,128]{1,0:T(8,128)S(1)}, u32[]{:S(2)}, u32[]{:S(2)}) collective-permute-start(f32[144,128]{1,0:T(8,128)S(1)} %branch_1_fun.3), channel_id=1, source_target_pairs={{0,1},{1,2},{2,3},{3,4},{4,5},{5,6},{6,7},{8,9},{9,10},{10,11},{11... | collective-permute-start | bytes 221192 | tf_op jit(solution)/shard_map/cond/branch_1_fun/ppermute | solution.py:578

commit v5 on v4

--- a/solution.py
+++ b/solution.py
@@ -277,6 +277,7 @@
     b_ref,
     p_ref,
     s_ref,
+    edge_ref,
     w_ref,
     ve_ref,
     vo_ref,
@@ -406,6 +407,8 @@
             if low <= start < high:
                 stage(start)
 
+    edges_kernel(b_ref, p_ref, s_ref, edge_ref)
+
     def total(x):
         return jnp.sum(jnp.sum(x, axis=0, keepdims=True), axis=1, keepdims=True)
 
@@ -565,24 +568,23 @@
     from_right = lax.ppermute(to_left, "axial", [(i + 1, i) for i in range(AN - 1)])
     cost = pl.CostEstimate(flops=2_000_000, bytes_accessed=4_000_000, transcendentals=0)
     own, flag = call(place_kernel, [(4, ROWS, 128)], n_in=1, cost=cost, flag=True)(b_own)
-    red, b, p, s = call(
+    red, b, p, s, edges = call(
         operate_kernel,
-        [(QN * AN, 8), (4, ROWS, 128), (4, ROWS, 128), (4, 256, 128)],
+        [(QN * AN, 8), (4, ROWS, 128), (4, ROWS, 128), (4, 256, 128), (144, 128)],
         OPERATE_SCRATCH,
         n_in=3,
     )(own, mask_cols, from_right)
     all_red = lax.all_to_all(red, ("circ", "axial"), 0, 0, tiled=True)
 
-    def share(b, p, s):
-        (edges,) = call(edges_kernel, [(144, 128)], n_in=3, cost=cost)(b, p, s)
+    def share(b, p, s, edges):
         edge = lax.ppermute(edges, "axial", [(i, i + 1) for i in range(AN - 1)])
         parts = call(unpack_kernel, [(KS, 256, 128)] * 3, n_in=3, cost=cost)(b, p, s)
         return tuple(call(merge_kernel, [(KS, 256, 128)] * 3, n_in=4, cost=cost)(edge, *parts))
 
-    def keep(b, p, s):
+    def keep(b, p, s, edges):
         return tuple(x[:KS, :256] for x in (b, p, s))
 
-    bm, pm, sm = lax.cond(flag[0] > 0, share, keep, b, p, s)
+    bm, pm, sm = lax.cond(flag[0] > 0, share, keep, b, p, s, edges)
     return tuple(call(finish_kernel, [(KS, 256, 128)] * 2, FINISH_SCRATCH, n_in=4, hbm_out=True)(all_red, bm, pm, sm))
 
 

time: 78 us -> 78.3 us (level)
  transfers between devices with their start and end apart: 3 -> 3, of which waited for: 3 -> 3; matrix products, arithmetic and copies ran while one was open for 0% -> 0% of each run, Pallas kernels for 3% -> 2%
where the time goes in v5:
time: 78.3 us; the launch traced here: 78 us
  blocking collectives  37.6 us (48%)
  starting transfers between devices  16.6 us (21%)
  Pallas kernels  11.6 us (15%)
  waiting for transfers between devices  10.9 us (14%)
  between operations  1.32 us (2%)
    all_to_all x1, blocking collectives, shards(): lax.all_to_all(packed.reshape(QN, PR, 128), 'circ', 0, 0, tiled=True)  37.6 us
    all_to_all x1, starting transfers between devices, shards(): all_red = lax.all_to_all(red, ('circ', 'axial'), 0, 0, tiled=True)  12 us
    all_to_all x1, waiting for transfers between devices, shards(): all_red = lax.all_to_all(red, ('circ', 'axial'), 0, 0, tiled=True)  6.92 us
    pallas_call x1, Pallas kernels, shards(): call(operate_kernel, [(QN * AN, 8), (4, ROWS, 128), (4, ROWS, 128), (4, 2...  4.83 us
    ppermute x1, starting transfers between devices, share(): edge = lax.ppermute(edges, 'axial', [(i, i + 1) for i in range(AN - 1)])  3.29 us
    ppermute x1, waiting for transfers between devices, shards(): lax.ppermute(to_left, 'axial', [(i + 1, i) for i in range(AN - 1)])  2.9 us
    pallas_call x1, Pallas kernels, shards(): call(pack_kernel, [(QN * PR, 128)], PACK_SCRATCH, n_in=2, hbm_in=True)  2.83 us
  transfers between devices with their start and end apart: 3, of which 3 were waited for; matrix products, arithmetic and copies ran while one was open for 0% of the time, Pallas kernels for 2%

profile of v5, /device:TPU:1, one launch (start us, length us, event | category | flops | bytes accessed | tf_op | source)
XLA Modules:
  0.0 78.0 jit_solution(6229736988673217730)
XLA Ops:
  0.6 2.8 %shard_map.41 = f32[1792,128]{1,0:T(8,128)S(1)} custom-call(s32[2,4]{1,0:T(2,128)} %bitcast.13, f32[3,1024,128]{2,1,0:T(8,128)} %bitcast.12), custom_call_target="tpu_custom_call" | custom-call | tf_op jit(solution)/shard_map/pallas_call | solution.py:561
  3.5 37.6 %all_to_all.16 = f32[32,56,128]{2,1,0:T(8,128)S(1)} all-to-all(f32[32,56,128]{2,1,0:T(8,128)S(1)} %bitcast.10), channel_id=1, replica_groups=mesh['circ'=32,'axial'=8] {'circ'}, dimensions={0} | all-to-all | bytes 1835008 | tf_op jit(solution)/shard_map/all_to_all | solution.py:562
  41.1 0.8 %shard_map.42 = (f32[4,288,128]{2,1,0:T(8,128)S(1)}, f32[144,128]{1,0:T(8,128)S(1)}, f32[8,128]{1,0:T(8,128)S(1)}) custom-call(f32[1792,128]{1,0:T(8,128)S(1)} %bitcast.9), custom_call_target="tpu_custom_call" | custom-call | tf_op jit(solution)/shard_map/pallas_call | solution.py:563
  41.9 1.3 %collective-permute-start.1 = (f32[144,128]{1,0:T(8,128)S(1)}, f32[144,128]{1,0:T(8,128)S(1)}, u32[]{:S(2)}, u32[]{:S(2)}) collective-permute-start(f32[144,128]{1,0:T(8,128)S(1)} %get-tuple-element.42), channel_id=1, source_target_pairs={{1,0},{2,1},{3,2},{4,3},{5,4},{6,5},{7,6},{9,8},{10,9},{11,10},{12... | collective-permute-start | bytes 221192 | tf_op jit(solution)/shard_map/ppermute | solution.py:568
  43.2 0.9 %shard_map.43 = (f32[4,288,128]{2,1,0:T(8,128)S(1)}, s32[1]{0:T(128)}) custom-call(f32[4,288,128]{2,1,0:T(8,128)S(1)} %get-tuple-element.39.b_ref), custom_call_target="tpu_custom_call" | custom-call | flops 2000000 | bytes 4000000 | tf_op jit(solution)/shard_map/pallas_call | solution.py:570
  44.1 2.9 %collective-permute-done.1.from_right_ref = f32[144,128]{1,0:T(8,128)S(1)} collective-permute-done((f32[144,128]{1,0:T(8,128)S(1)}, f32[144,128]{1,0:T(8,128)S(1)}, u32[]{:S(2)}, u32[]{:S(2)}) %collective-permute-start.1) | collective-permute-done | bytes 73760 | tf_op jit(solution)/shard_map/ppermute | solution.py:568
  47.0 4.8 %shard_map.44 = (f32[256,8]{1,0:T(8,128)}, f32[4,288,128]{2,1,0:T(8,128)S(1)}, f32[4,288,128]{2,1,0:T(8,128)S(1)}, f32[4,256,128]{2,1,0:T(8,128)S(1)}, f32[144,128]{1,0:T(8,128)S(1)}) custom-call(f32[4,288,128]{2,1,0:T(8,128)S(1)} %get-tuple-element.40.own_ref, f32[8,128]{1,0:T(8,128)S(1)} %get-tuple-element.41.m_ref, ...), custom_call_target="tpu_custom_call" | custom-call | tf_op jit(solution)/shard_map/pallas_call | solution.py:571
  51.8 12.0 %all-to-all-start.1 = ((f32[256,1,8]{2,1,0:T(1,128)}), f32[256,1,8]{2,1,0:T(1,128)S(1)}, u32[]{:S(2)}, u32[]{:S(2)}) async-start(f32[256,1,8]{2,1,0:T(1,128)} %bitcast.5), calls=%async_computation.1 | async-start | bytes 262144 | tf_op jit(solution)/shard_map/all_to_all | solution.py:577
  64.5 5.1 %conditional.1 = ((f32[3,256,128]{2,1,0:T(8,128)S(1)}, f32[3,256,128]{2,1,0:T(8,128)S(1)}, f32[3,256,128]{2,1,0:T(8,128)S(1)})) conditional(s32[]{:T(128)} %bitcast.7, (f32[4,288,128]{2,1,0:T(8,128)S(1)}, f32[4,288,128]{2,1,0:T(8,128)S(1)}, f32[4,256,128]{2,1,0:T(8,128)S(1)}) %tuple.14, (f32[144,128]{1,0:T(8,128)S(1)}, f32[4,288,128]{2,1,0:T(8,128)S(1)}, ...), branch_computations={%region_0.0_spmd, %region_1.0_spmd} | conditional | flops 4000000 | bytes 8294960 | solution.py:587
  64.5 3.3 %collective-permute-start = (f32[144,128]{1,0:T(8,128)S(1)}, f32[144,128]{1,0:T(8,128)S(1)}, u32[]{:S(2)}, u32[]{:S(2)}) collective-permute-start(f32[144,128]{1,0:T(8,128)S(1)} %get-tuple-element.17), channel_id=1, source_target_pairs={{0,1},{1,2},{2,3},{3,4},{4,5},{5,6},{6,7},{8,9},{9,10},{10,11},{11... | collective-permute-start | bytes 221192 | tf_op jit(solution)/shard_map/cond/branch_1_fun/ppermute | solution.py:580
  67.8 0.4 branch_1_fun.2
  68.2 1.1 %collective-permute-done.edge_ref = f32[144,128]{1,0:T(8,128)S(1)} collective-permute-done((f32[144,128]{1,0:T(8,128)S(1)}, f32[144,128]{1,0:T(8,128)S(1)}, u32[]{:S(2)}, u32[]{:S(2)}) %collective-permute-start) | collective-permute-done | bytes 73760 | tf_op jit(solution)/shard_map/cond/branch_1_fun/ppermute | solution.py:580
  69.3 0.3 branch_1_fun.3
  69.6 6.9 %all-to-all-done.1 = f32[256,1,8]{2,1,0:T(1,128)S(1)} async-done(((f32[256,1,8]{2,1,0:T(1,128)}), f32[256,1,8]{2,1,0:T(1,128)S(1)}, u32[]{:S(2)}, u32[]{:S(2)}) %all-to-all-start.1) | async-done | bytes 8224 | tf_op jit(solution)/shard_map/all_to_all | solution.py:577
  76.5 1.5 %shard_map.45 = (f32[3,256,128]{2,1,0:T(8,128)}, f32[3,256,128]{2,1,0:T(8,128)}) custom-call(f32[256,8]{1,0:T(8,128)S(1)} %bitcast.11, f32[3,256,128]{2,1,0:T(8,128)S(1)} %get-tuple-element.49.b_ref, f32[3,256,128]{2,1,0:T(8,128)S(1)} %get-tuple-element.50.p_ref, f32[3,256,128]{2,1,0:T(8,128)S(1)} %get-tuple-element.51.s_ref), custom_call_target="tpu_custom_call" | custom-call | tf_op jit(solution)/shard_map/pallas_call | solution.py:588
Async XLA Ops:
  41.9 5.1 %collective-permute-start.1 = (f32[144,128]{1,0:T(8,128)S(1)}, f32[144,128]{1,0:T(8,128)S(1)}, u32[]{:S(2)}, u32[]{:S(2)}) collective-permute-start(f32[144,128]{1,0:T(8,128)S(1)} %get-tuple-element.42), channel_id=1, source_target_pairs={{1,0},{2,1},{3,2},{4,3},{5,4},{6,5},{7,6},{9,8},{10,9},{11,10},{12... | collective-permute-start | bytes 221192 | tf_op jit(solution)/shard_map/ppermute | solution.py:568
  51.8 24.7 %all-to-all-start.1 = ((f32[256,1,8]{2,1,0:T(1,128)}), f32[256,1,8]{2,1,0:T(1,128)S(1)}, u32[]{:S(2)}, u32[]{:S(2)}) async-start(f32[256,1,8]{2,1,0:T(1,128)} %bitcast.5), calls=%async_computation.1 | async-start | bytes 262144 | tf_op jit(solution)/shard_map/all_to_all | solution.py:577
  64.5 4.8 %collective-permute-start = (f32[144,128]{1,0:T(8,128)S(1)}, f32[144,128]{1,0:T(8,128)S(1)}, u32[]{:S(2)}, u32[]{:S(2)}) collective-permute-start(f32[144,128]{1,0:T(8,128)S(1)} %get-tuple-element.17), channel_id=1, source_target_pairs={{0,1},{1,2},{2,3},{3,4},{4,5},{5,6},{6,7},{8,9},{9,10},{10,11},{11... | collective-permute-start | bytes 221192 | tf_op jit(solution)/shard_map/cond/branch_1_fun/ppermute | solution.py:580
